TPU v7x, 32 devices: a whole 2x2x4 slice. The times are simulated.
32 devices in a mesh: row: 16 (over z, y, core), col: 2 (over x).
Axes of the slice: x: 2, y: 2, z: 4, core: 2. Of those that a mesh axis runs over, the one named last changes fastest.
Arguments:
- half_slab: bfloat16 [11264, 4608], P(('row', 'col')), may hold values from -6 to 6
- coef: bfloat16 [4608, 4096], P('row', 'col'), may hold values from -0.01171875 to 0.01171875
- virt_energy: float32 [4096], replicated, may hold values from 0.1 to 4
- occ_energy: float32 [1], replicated, may hold values from -1 to -0.4
- frequency: float32 [3], replicated, may hold values from 0.05 to 3
Outputs:
- polar: float32 [3, 11264, 11264], P(None, 'row', 'col')
All inputs are finite; a program needn't handle non-finite values.
Results may differ from a plain program's by a relative error of at most 0.0035.
Values may be sent and summed in bfloat16 or wider, within the bound.
No kernel may reach another device: no remote copies, remote signals or barrier semaphores. Data moves between devices by JAX's collectives and lax.ppermute only.
A program may use at most 320 MiB of HBM per device.

v0:
```python
import jax
import jax.numpy as jnp
from jax import lax
from jax.sharding import PartitionSpec as P


def shards(half_slab, coef, virt_energy, occ_energy, frequency):
    slab_rows = lax.all_gather(half_slab, "col", axis=0, tiled=True)
    local_block = jnp.dot(
        slab_rows,
        lax.all_gather(coef, "row", axis=0, tiled=True),
        preferred_element_type=jnp.float32,
    ).astype(jnp.bfloat16)
    row_panel = lax.all_gather(local_block, "col", axis=1, tiled=True)
    column_all = lax.all_gather(local_block, "row", axis=0, tiled=True)
    partner = lax.all_to_all(column_all, "col", split_axis=0, concat_axis=1, tiled=True)
    energy_gap = virt_energy - occ_energy[0]
    results = []
    for index in range(frequency.shape[0]):
        weights = 2.0 * energy_gap / (energy_gap * energy_gap + frequency[index] * frequency[index])
        scaled = (row_panel.astype(jnp.float32) * weights[None, :]).astype(jnp.bfloat16)
        results.append(
            lax.dot_general(
                scaled, partner, (((1,), (1,)), ((), ())), preferred_element_type=jnp.float32
            )
        )
    return jnp.stack(results, 0)


def solution(mesh):
    in_specs = (P(("row", "col"), None), P("row", "col"), P(), P(), P())
    out_specs = P(None, "row", "col")
    return jax.shard_map(shards, mesh=mesh, in_specs=in_specs, out_specs=out_specs, check_vma=False)
```

profile of v0, /device:TPU:2, one launch (start us, length us, event | category | flops | bytes accessed | tf_op | source)
XLA Modules:
  0.0 1236.2 jit_solution(10686772049038704836)
XLA Ops:
  6.5 0.0 all-gather.5.cloned.1.call-start
  6.5 0.7 all-gather.5.cloned.1.call-update
  7.3 0.0 all-gather.7.cloned.1.call-start
  7.3 0.7 all-gather.7.cloned.1.call-update
  8.0 0.0 all-gather.11.cloned.1.call-start
  8.1 83.5 %all-gather.5.cloned.1.call-done = bf16[704,4608]{1,0:T(8,128)(2,1)} async-done(((bf16[352,4608]{1,0:T(8,128)(2,1)}), bf16[704,4608]{1,0:T(8,128)(2,1)}) %all-gather.5.cloned.1.call-update) | async-done | bytes 6488080 | tf_op jit(solution)/shard_map/all_gather | solution.py:8
  91.6 101.7 %all-gather.7.cloned.1.call-done = bf16[4608,2048]{1,0:T(8,128)(2,1)} async-done(((bf16[288,2048]{1,0:T(8,128)(2,1)}), bf16[4608,2048]{1,0:T(8,128)(2,1)}) %all-gather.7.cloned.1.call-update) | async-done | bytes 18874384 | tf_op jit(solution)/shard_map/all_gather | solution.py:11
  193.3 20.4 %convolution_convert_fusion = bf16[704,2048]{1,0:T(8,128)(2,1)} fusion(bf16[704,4608]{1,0:T(8,128)(2,1)} %all-gather.5.cloned.1.call-done, bf16[4608,2048]{1,0:T(8,128)(2,1)} %all-gather.7.cloned.1.call-done), kind=kOutput, calls=%fused_computation.13 | convolution fusion | flops 13288996864 | bytes 28246016 | tf_op jit(solution)/shard_map/dot_general | solution.py:9
  213.7 0.0 all-gather.11.cloned.1.call-update
  213.8 227.5 %all-gather.11.cloned.1.call-done = bf16[11264,2048]{1,0:T(8,128)(2,1)} async-done(((bf16[704,2048]{1,0:T(8,128)(2,1)}), bf16[11264,2048]{1,0:T(8,128)(2,1)}) %all-gather.11.cloned.1.call-update) | async-done | bytes 46137360 | tf_op jit(solution)/shard_map/all_gather | solution.py:15
  441.2 55.1 %copy.6 = bf16[2,5632,2048]{1,2,0:T(8,128)(2,1)} copy(bf16[2,5632,2048]{2,1,0:T(8,128)(2,1)} %bitcast.20) | data formatting | bytes 92274688 | tf_op jit(solution)/shard_map/all_to_all | solution.py:16
  496.3 0.0 copy-start.1
  496.3 18.7 %all-to-all-start = ((bf16[2,5632,2048]{1,2,0:T(8,128)(2,1)}), bf16[2,5632,2048]{1,2,0:T(8,128)(2,1)}, u32[]{:S(2)}, u32[]{:S(2)}) async-start(bf16[2,5632,2048]{1,2,0:T(8,128)(2,1)} %copy.6), calls=%async_computation | async-start | bytes 92274688 | tf_op jit(solution)/shard_map/all_to_all | solution.py:16
  515.1 0.0 all-gather.9.cloned.1.call-start
  515.1 0.6 all-gather.9.cloned.1.call-update
  516.3 0.0 copy-done.1
  516.3 0.6 fusion.9
  520.6 0.0 copy-done
  520.7 131.7 %all-gather.9.cloned.1.call-done = bf16[704,4096]{1,0:T(8,128)(2,1)} async-done(((bf16[704,2048]{1,0:T(8,128)(2,1)}), bf16[704,4096]{1,0:T(8,128)(2,1)}) %all-gather.9.cloned.1.call-update) | async-done | bytes 5767184 | tf_op jit(solution)/shard_map/all_gather | solution.py:14
  652.4 420.3 %all-to-all-done = bf16[2,5632,2048]{1,2,0:T(8,128)(2,1)} async-done(((bf16[2,5632,2048]{1,2,0:T(8,128)(2,1)}), bf16[2,5632,2048]{1,2,0:T(8,128)(2,1)}, u32[]{:S(2)}, u32[]{:S(2)}) %all-to-all-start) | async-done | bytes 46137376 | tf_op jit(solution)/shard_map/all_to_all | solution.py:16
  1072.6 41.8 %convolution_bitcast_fusion.2 = f32[1,704,5632]{2,1,0:T(8,128)} fusion(bf16[5632,4096]{0,1:T(8,128)(2,1)} %bitcast.4, bf16[704,4096]{1,0:T(8,128)(2,1)} %all-gather.9.cloned.1.call-done, f32[4096]{0:T(1024)S(1)} %get-tuple-element.5), kind=kOutput, calls=%fused_computation.9 | convolution fusion | flops 32489340928 | bytes 67780608 | tf_op jit(solution)/shard_map/dot_general | solution.py:23
  1114.4 41.8 %convolution_bitcast_fusion = f32[1,704,5632]{2,1,0:T(8,128)} fusion(bf16[5632,4096]{0,1:T(8,128)(2,1)} %bitcast.4, bf16[704,4096]{1,0:T(8,128)(2,1)} %all-gather.9.cloned.1.call-done, f32[4096]{0:T(1024)S(1)} %get-tuple-element.6), kind=kOutput, calls=%fused_computation.7 | convolution fusion | flops 32489340928 | bytes 67780608 | tf_op jit(solution)/shard_map/dot_general | solution.py:23
  1156.3 41.8 %convolution_bitcast_fusion.1 = f32[1,704,5632]{2,1,0:T(8,128)} fusion(bf16[5632,4096]{0,1:T(8,128)(2,1)} %bitcast.4, bf16[704,4096]{1,0:T(8,128)(2,1)} %all-gather.9.cloned.1.call-done, f32[4096]{0:T(1024)S(1)} %get-tuple-element.7), kind=kOutput, calls=%fused_computation.8 | convolution fusion | flops 32489340928 | bytes 67780608 | tf_op jit(solution)/shard_map/dot_general | solution.py:23
  1198.1 31.6 %pad_maximum_fusion = f32[3,704,5632]{2,1,0:T(8,128)} fusion(f32[1,704,5632]{2,1,0:T(8,128)} %convolution_bitcast_fusion, f32[1,704,5632]{2,1,0:T(8,128)} %convolution_bitcast_fusion.1, f32[1,704,5632]{2,1,0:T(8,128)} %convolution_bitcast_fusion.2), kind=kLoop, calls=%fused_computation | loop fusion | flops 23789568 | bytes 95158272 | tf_op jit(solution)/shard_map/stack | solution.py:27
  (2 shorter events, 0.0 us)
Async XLA Ops:
  6.5 85.1 %all-gather.5.cloned.1.call-start = ((), (), s32[]{:S(2)}) async-start(), calls=%async_computation.1 | async-start | bytes 9732096 | tf_op jit(solution)/shard_map/all_gather | solution.py:8
  7.3 186.1 %all-gather.7.cloned.1.call-start = ((), (), s32[]{:S(2)}) async-start(), calls=%async_computation.2 | async-start | bytes 20054016 | tf_op jit(solution)/shard_map/all_gather | solution.py:11
  8.0 433.2 %all-gather.11.cloned.1.call-start = ((), (), s32[]{:S(2)}) async-start(), calls=%async_computation.4 | async-start | bytes 49020928 | tf_op jit(solution)/shard_map/all_gather | solution.py:15
  496.3 19.9 %copy-start.1 = (f32[3]{0:T(128)S(1)}, f32[3]{0:T(128)}, u32[]{:S(2)}) copy-start(f32[3]{0:T(128)} %param.9) | copy-start | bytes 40
  496.3 24.3 %copy-start = (f32[4096]{0:T(1024)S(1)}, f32[4096]{0:T(1024)}, u32[]{:S(2)}) copy-start(f32[4096]{0:T(1024)} %param.7) | copy-start | bytes 49156
  496.3 576.3 %all-to-all-start = ((bf16[2,5632,2048]{1,2,0:T(8,128)(2,1)}), bf16[2,5632,2048]{1,2,0:T(8,128)(2,1)}, u32[]{:S(2)}, u32[]{:S(2)}) async-start(bf16[2,5632,2048]{1,2,0:T(8,128)(2,1)} %copy.6), calls=%async_computation | async-start | bytes 92274688 | tf_op jit(solution)/shard_map/all_to_all | solution.py:16
  515.1 137.3 %all-gather.9.cloned.1.call-start = ((), (), s32[]{:S(2)}) async-start(), calls=%async_computation.3 | async-start | bytes 8650752 | tf_op jit(solution)/shard_map/all_gather | solution.py:14
Sparse Core Ops, SparseCore 0:
  8.9 82.6 all-gather.4
  93.2 100.1 all-gather.6
  213.9 227.3 all-gather.10
  517.1 135.2 all-gather.8
where the time goes:
time: 1240 us
  waiting for transfers between devices  967 us (78%)
  matrix products  146 us (12%)
  local copies, waits for them, and re-layouts  55.7 us (4%)
  other arithmetic  31.6 us (3%)
  starting transfers between devices  18.8 us (2%)
  between operations  17.5 us (1%)
    all_to_all x1, waiting for transfers between devices, shards(): lax.all_to_all(column_all, 'col', split_axis=0, concat_axis=1, tiled=True)  420 us
    all_gather x1, waiting for transfers between devices, shards(): column_all = lax.all_gather(local_block, 'row', axis=0, tiled=True)  227 us
    all_gather x1, waiting for transfers between devices, shards(): row_panel = lax.all_gather(local_block, 'col', axis=1, tiled=True)  132 us
    dot_general x3, matrix products, shards(): lax.dot_general(scaled, partner, (((1,), (1,)), ((), ())), preferred_elem...  125 us
    all_gather x1, waiting for transfers between devices, shards(): lax.all_gather(coef, 'row', axis=0, tiled=True)  102 us
    all_gather x1, waiting for transfers between devices, shards(): slab_rows = lax.all_gather(half_slab, 'col', axis=0, tiled=True)  83.5 us
    all_to_all x1, local copies, waits for them, and re-layouts, shards(): lax.all_to_all(column_all, 'col', split_axis=0, concat_axis=1, tiled=True)  55.1 us
    another operation x1, other arithmetic, shards(): return jnp.stack(results, 0)  31.6 us
  transfers between devices with their start and end apart: 5, of which 5 were waited for; matrix products, arithmetic and copies ran while one was open for 0% of the time, Pallas kernels for 0%

commit v1 on v0

v1 whole, which is shorter than its diff:
```python
import functools

import jax
import jax.numpy as jnp
from jax import lax
from jax.experimental import pallas as pl
from jax.experimental.pallas import tpu as pltpu
from jax.sharding import PartitionSpec as P

AXES = ("row", "col")
BF16, F32 = jnp.bfloat16, jnp.float32
SLAB_PARTS = 5
PARTS = 2


def all_weights(virt_energy, occ_energy, frequency):
    gap = virt_energy - occ_energy[0]
    return 2.0 * gap[None] / (gap[None] * gap[None] + frequency[:, None] * frequency[:, None])


def gathered(half_slab, coef, virt_energy, occ_energy, frequency):
    slab_rows = lax.all_gather(half_slab, "col", axis=0, tiled=True)
    coef_all = lax.all_gather(coef, "row", axis=0, tiled=True)
    block = jnp.dot(slab_rows, coef_all, preferred_element_type=F32).astype(BF16)
    row_panel = lax.all_gather(block, "col", axis=1, tiled=True)
    column_all = lax.all_gather(block, "row", axis=0, tiled=True)
    partner = lax.all_to_all(column_all, "col", split_axis=0, concat_axis=1, tiled=True)
    weights = all_weights(virt_energy, occ_energy, frequency)
    scaled = (row_panel.astype(F32)[None] * weights[:, None, :]).astype(BF16)
    return lax.dot_general(scaled, partner, (((2,), (1,)), ((), ())), preferred_element_type=F32)


def block_kernel(place, scaled, *refs, first):
    pieces, out = refs[:4], refs[-1]
    width = pieces[0].shape[1]
    total = None
    for i, piece in enumerate(pieces):
        term = lax.dot_general(
            scaled[0, :, i * width : (i + 1) * width],
            piece[...],
            (((1,), (1,)), ((), ())),
            preferred_element_type=F32,
        )
        total = term if total is None else total + term
    out[0] = total if first else total + refs[4][0]


def add_block(out, shape, place, scaled, pieces, first):
    freqs, rows, depth = scaled.shape
    cols, width = pieces[0].shape
    tile = rows // 2
    block = pl.BlockSpec((1, tile, cols), lambda f, i, p: (f, i, p[0]))
    in_specs = [pl.BlockSpec((1, tile, depth), lambda f, i, p: (f, i, 0))]
    in_specs += [pl.BlockSpec((cols, width), lambda f, i, p: (0, 0))] * 4
    operands, aliases = [place.reshape(1).astype(jnp.int32), scaled, *pieces], {}
    if out is not None:
        in_specs.append(pl.BlockSpec(memory_space=pl.ANY) if first else block)
        operands.append(out)
        aliases = {6: 0}
    return pl.pallas_call(
        functools.partial(block_kernel, first=first),
        out_shape=jax.ShapeDtypeStruct(shape, F32),
        grid_spec=pltpu.PrefetchScalarGridSpec(
            num_scalar_prefetch=1, grid=(freqs, 2), in_specs=in_specs, out_specs=block
        ),
        input_output_aliases=aliases,
        compiler_params=pltpu.CompilerParams(vmem_limit_bytes=56 * 2**20),
        cost_estimate=pl.CostEstimate(
            flops=2 * freqs * rows * cols * depth,
            bytes_accessed=4 * (2 - first) * freqs * rows * cols + 2 * depth * (freqs * rows + cols),
            transcendentals=0,
        ),
    )(*operands)


def line_plan(half_slab, coef, virt_energy, occ_energy, frequency):
    row, x = lax.axis_index("row"), lax.axis_index("col")
    z, y, k = row // 4, (row // 2) % 2, row % 2
    u = jnp.where(x == 0, z, 3 - z)

    def device(z, y, k, x):
        return ((z * 2 + y) * 2 + k) * 2 + x

    def move(array, target):
        pairs = []
        for dz in range(4):
            for dy in range(2):
                for dk in range(2):
                    for dx in range(2):
                        to = target(dz, dy, dk, dx)
                        if to is not None:
                            pairs.append((device(dz, dy, dk, dx), device(*to)))
        return lax.ppermute(array, AXES, pairs)

    def over_x(a):
        return move(a, lambda z, y, k, x: (z, y, k, 1 - x))

    def over_y(a):
        return move(a, lambda z, y, k, x: (z, 1 - y, k, x))

    def over_k(a):
        return move(a, lambda z, y, k, x: (z, y, 1 - k, x))

    def z_up(a, step):
        return move(a, lambda z, y, k, x: (z + 1, y, k, x) if step - 1 <= z < 3 else None)

    def z_down(a, step):
        return move(a, lambda z, y, k, x: (z - 1, y, k, x) if 0 < z <= 4 - step else None)

    def u_to(a, steps):
        def target(z, y, k, x):
            u = z if x == 0 else 3 - z
            if u not in steps:
                return None
            v = steps[u]
            return (v if x == 0 else 3 - v), y, k, x

        return move(a, target)

    slab_rows, nao = half_slab.shape
    chip_rows = 4 * slab_rows
    rows = chip_rows // 2
    coef_rows, virt_x = coef.shape
    both = virt_x // PARTS
    width = both // 2
    weights = all_weights(virt_energy, occ_energy, frequency)
    freqs = weights.shape[0]
    shape = (freqs, rows, 4 * chip_rows)

    env = {}

    def step(**results):
        env.update(results)
        names = list(env)
        env.update(zip(names, lax.optimization_barrier([env[n] for n in names])))

    def slot(c, n):
        up = [None] + [env.get(f"up{c}{i}") for i in (1, 2, 3)]
        down = [None] + [env.get(f"down{c}{i}") for i in (1, 2, 3)]
        if n == 0:
            return env[f"coef{c}"]
        if n == 1:
            return jnp.where(z == 0, down[1], up[1])
        if n == 2:
            return jnp.where(z == 0, down[2], jnp.where(z == 3, up[2], down[1]))
        return jnp.where(z == 0, down[3], jnp.where(z == 1, down[2], jnp.where(z == 2, up[2], up[3])))

    planes = (
        z,
        jnp.where(z == 0, 1, z - 1),
        jnp.where(z == 0, 2, jnp.where(z == 3, 1, z + 1)),
        jnp.where(z <= 1, 3, 0),
    )

    def line(c, i):
        before = (env[f"coef{c}"],) * 2 if i == 1 else (env[f"up{c}{i - 1}"], env[f"down{c}{i - 1}"])
        return {f"up{c}{i}": z_up(before[0], i), f"down{c}{i}": z_down(before[1], i)}

    def cross(c, n):
        piece = slot(c, n)
        return {f"slot{c}{n}": piece, f"cross{c}{n}": over_y(piece)}

    def cores(c):
        mine = jnp.zeros((8, coef_rows, both), BF16)
        for n in range(4):
            mine = lax.dynamic_update_slice(mine, env.pop(f"slot{c}{n}")[None], (planes[n] * 2 + y, 0, 0))
            mine = lax.dynamic_update_slice(mine, env.pop(f"cross{c}{n}")[None], (planes[n] * 2 + 1 - y, 0, 0))
        theirs = over_k(lax.dynamic_slice(mine, (0, 0, (1 - k) * width), (8, coef_rows, width)))
        return {f"keep{c}": lax.dynamic_slice(mine, (0, 0, k * width), (8, coef_rows, width)), f"theirs{c}": theirs}

    def transformed(c):
        keep, theirs = env.pop(f"keep{c}"), env.pop(f"theirs{c}")
        whole = jnp.where(k == 0, jnp.stack([keep, theirs], 1), jnp.stack([theirs, keep], 1)).reshape(nao, width)
        return {f"own{c}0": jnp.dot(env["slab"], whole, preferred_element_type=F32).astype(BF16)}

    def chip_slab():
        slab = jnp.zeros((4, slab_rows, nao), BF16)
        for name, at in (
            ("slab_o", k * 2 + x),
            ("slab_k", (1 - k) * 2 + x),
            ("slab_x", k * 2 + 1 - x),
            ("slab_kx", (1 - k) * 2 + 1 - x),
        ):
            slab = lax.dynamic_update_slice(slab, env.pop(name)[None], (at, 0, 0))
        return {"slab": slab.reshape(chip_rows, nao)}

    def panel(c):
        parts = []
        for p, v in ((0, x), (1, 1 - x)):
            for held, core in ((env[f"own{c}{p}"], k), (env.pop(f"kown{c}{p}"), 1 - k)):
                of_rows = lax.dynamic_slice(held, (k * rows, 0), (rows, width))
                at = v * virt_x + c * both + core * width
                scale = lax.dynamic_slice(weights, (0, at), (freqs, width))
                parts.append((of_rows.astype(F32)[None] * scale[:, None]).astype(BF16))
        return {f"scaled{c}": jnp.concatenate(parts, 2)}

    items = [(c, near, p) for c in range(PARTS) for near in (1, 0) for p in (0, 1)]
    count = len(items)

    def item(t):
        c, near, p = items[t]
        return env[f"own{c}{p}"] if near else env[f"far{c}{p}"]

    def exchange(c, p):
        return {f"far{c}{p}": u_to(env[f"own{c}{p}"], {0: 1, 1: 0})}

    def along(t):
        if t == 0:
            return {"got0": u_to(item(0), {1: 2})}
        if t == count:
            return {f"got{t}": u_to(env[f"got{t - 1}"], {2: 3})}
        return {f"got{t}": u_to(jnp.where(u == 1, item(t), env[f"got{t - 1}"]), {1: 2, 2: 3})}

    def take(t):
        held = jnp.where(u <= 1, item(t), jnp.where(u == 2, env[f"got{t}"], env[f"got{t + 1}"]))
        return {f"a{t}": held, f"b{t}": over_y(held), f"ka{t}": over_k(held)}

    def take_k(t):
        return {f"kb{t}": over_k(env[f"b{t}"])}

    def block(t, crossed):
        c, near, _ = items[t]
        plane = jnp.where(u == 0, 1 - near, near)
        plane = jnp.where(x == 0, plane, 1 - plane)
        place = plane * 2 + (1 - y if crossed else y)
        s = "b" if crossed else "a"
        pieces = [env.pop(f"{h}{s}{i}") for i in (t, t + 1) for h in ("", "k")]
        env["out"] = add_block(env.get("out"), shape, place, env[f"scaled{c}"], pieces, c == 0)

    for c in range(PARTS):
        env[f"coef{c}"] = coef[:, c * both : (c + 1) * both]
    env["slab_o"] = half_slab
    step()
    cuts = [slab_rows * i // SLAB_PARTS // 16 * 16 for i in range(SLAB_PARTS)] + [slab_rows]

    def slab_part(i):
        return {f"slab_x{i}": over_x(env["slab_o"][cuts[i] : cuts[i + 1]])}

    step(**line(0, 1), **cross(0, 0), **slab_part(0), slab_k=over_k(env["slab_o"]))
    step(**line(0, 2), **cross(0, 1), **slab_part(1))
    step(**line(0, 3), **cross(0, 2), **slab_part(2))
    step(**line(1, 1), **cross(0, 3), **slab_part(3))
    step(**line(1, 2), **cross(1, 0), **cores(0), **slab_part(4))
    env["slab_x"] = jnp.concatenate([env.pop(f"slab_x{i}") for i in range(SLAB_PARTS)], 0)
    step(**line(1, 3), **cross(1, 1), slab_kx=over_k(env["slab_x"]))
    env.update(chip_slab())
    step(**transformed(0))
    step(**cross(1, 2), own01=over_x(env["own00"]), kown00=over_k(env["own00"]), **exchange(0, 0), **along(0))
    step(**cross(1, 3), kown01=over_k(env["own01"]), **exchange(0, 1), **along(1))
    step(**along(2), **take(0), **panel(0), **cores(1))
    r = along(3) | take(1) | take_k(0)
    env.update(transformed(1))
    step(**r)
    for t in range(2, count + 1):
        r = take(t) if t < count else {}
        r |= take_k(t - 1)
        if t + 2 <= count:
            r |= along(t + 2)
        if t == 2:
            r |= dict(own11=over_x(env["own10"]), kown10=over_k(env["own10"])) | exchange(1, 0)
        if t == 3:
            r |= dict(kown11=over_k(env["own11"])) | exchange(1, 1)
        if t == 4:
            r |= panel(1)
        if t % 2 == 0:
            block(t - 2, False)
        elif t > 2:
            block(t - 3, True)
        step(**r)
    block(count - 2, True)
    return env["out"]


def solution(mesh):
    in_specs = (P(("row", "col"), None), P("row", "col"), P(), P(), P())
    out_specs = P(None, "row", "col")
    lines = mesh.shape["row"] == 16 and mesh.shape["col"] == 2
    body = line_plan if lines else gathered
    return jax.shard_map(body, mesh=mesh, in_specs=in_specs, out_specs=out_specs, check_vma=False)
```

time: 1240 us -> 694 us (0.56)
  waiting for transfers between devices: 967 us -> 333 us
  Pallas kernels: 0 us -> 158 us
  matrix products: 146 us -> 19.6 us
  starting transfers between devices: 18.8 us -> 67.4 us
  between operations: 17.5 us -> 2.05 us
    all_gather x4 -> x0, waiting for transfers between devices: 544 us -> none  [the longest x1 227 us: shards(): column_all = lax.all_gather(local_block, 'row', axis=0, tiled=True)]
    all_to_all x1 -> x0, waiting for transfers between devices: 420 us -> none  [shards(): lax.all_to_all(column_all, 'col', split_axis=0, concat_axis=1, tiled=True)]
    ppermute x0 -> x72, waiting for transfers between devices: none -> 333 us  [move(): return lax.ppermute(array, AXES, pairs)]
    pallas_call x0 -> x8, Pallas kernels: none -> 158 us  [add_block(): pl.pallas_call(functools.partial(block_kernel, first=first), out_shape=ja...]
    dot_general x4 -> x2, matrix products: 146 us -> 19.6 us  [transformed(): jnp.dot(env['slab'], whole, preferred_element_type=F32).astype(BF16)]
    ppermute x0 -> x72, starting transfers between devices: none -> 67.4 us  [move(): return lax.ppermute(array, AXES, pairs)]
    all_to_all x1 -> x0, local copies, waits for them, and re-layouts: 55.1 us -> none  [shards(): lax.all_to_all(column_all, 'col', split_axis=0, concat_axis=1, tiled=True)]
    another operation x1 -> x0, other arithmetic: 31.6 us -> none  [shards(): return jnp.stack(results, 0)]
  transfers between devices with their start and end apart: 5 -> 72, of which waited for: 5 -> 30; matrix products, arithmetic and copies ran while one was open for 0% -> 8% of each run, Pallas kernels for 0% -> 20%
where the time goes in v1:
time: 694 us; the launch traced here: 684 us
  waiting for transfers between devices  333 us (48%)
  Pallas kernels  158 us (23%)
  starting transfers between devices  67.4 us (10%)
  local copies, waits for them, and re-layouts  60.3 us (9%)
  other arithmetic  43 us (6%)
  matrix products  19.6 us (3%)
    ppermute x72, waiting for transfers between devices, move(): return lax.ppermute(array, AXES, pairs)  333 us
    pallas_call x8, Pallas kernels, add_block(): pl.pallas_call(functools.partial(block_kernel, first=first), out_shape=ja...  158 us
    ppermute x72, starting transfers between devices, move(): return lax.ppermute(array, AXES, pairs)  67.4 us
    dot_general x2, matrix products, transformed(): jnp.dot(env['slab'], whole, preferred_element_type=F32).astype(BF16)  19.6 us
  transfers between devices with their start and end apart: 72, of which 30 were waited for; matrix products, arithmetic and copies ran while one was open for 8% of the time, Pallas kernels for 20%

profile of v1, /device:TPU:2, one launch (start us, length us, event | category | flops | bytes accessed | tf_op | source)
XLA Modules:
  0.0 683.9 jit_solution(11383087295916441473)
XLA Ops:
  33.7 13.4 %collective-permute-done.6 = bf16[288,1024]{1,0:T(8,128)(2,1)} collective-permute-done((bf16[288,1024]{1,0:T(8,128)(2,1)}, bf16[288,1024]{1,0:T(8,128)(2,1)}, u32[]{:S(2)}, u32[]{:S(2)}) %collective-permute-start.6) | collective-permute-done | bytes 589856 | tf_op jit(solution)/shard_map/ppermute | solution.py:93
  55.4 10.4 %collective-permute-done.10 = bf16[288,1024]{1,0:T(8,128)(2,1)} collective-permute-done((bf16[288,1024]{1,0:T(8,128)(2,1)}, bf16[288,1024]{1,0:T(8,128)(2,1)}, u32[]{:S(2)}, u32[]{:S(2)}) %collective-permute-start.10) | collective-permute-done | bytes 589856 | tf_op jit(solution)/shard_map/ppermute | solution.py:93
  108.1 18.4 %collective-permute-done.18 = bf16[288,1024]{1,0:T(8,128)(2,1)} collective-permute-done((bf16[288,1024]{1,0:T(8,128)(2,1)}, bf16[288,1024]{1,0:T(8,128)(2,1)}, u32[]{:S(2)}, u32[]{:S(2)}) %collective-permute-start.18) | collective-permute-done | bytes 589856 | tf_op jit(solution)/shard_map/ppermute | solution.py:93
  141.7 14.2 %collective-permute-done.23 = bf16[288,1024]{1,0:T(8,128)(2,1)} collective-permute-done((bf16[288,1024]{1,0:T(8,128)(2,1)}, bf16[288,1024]{1,0:T(8,128)(2,1)}, u32[]{:S(2)}, u32[]{:S(2)}) %collective-permute-start.23) | collective-permute-done | bytes 589856 | tf_op jit(solution)/shard_map/ppermute | solution.py:93
  177.4 10.7 %convolution_convert_fusion.1 = bf16[1408,512]{1,0:T(8,128)(2,1)} fusion(bf16[1408,4608]{1,0:T(8,128)(2,1)} %bitcast.57, bf16[4608,512]{1,0:T(8,128)(2,1)S(1)} %bitcast.64), kind=kOutput, calls=%fused_computation.17 | convolution fusion | flops 6644498432 | bytes 19136512 | tf_op jit(solution)/shard_map/dot_general | solution.py:174
  194.8 14.6 %collective-permute-done.26 = bf16[288,1024]{1,0:T(8,128)(2,1)} collective-permute-done((bf16[288,1024]{1,0:T(8,128)(2,1)S(1)}, bf16[288,1024]{1,0:T(8,128)(2,1)}, u32[]{:S(2)}, u32[]{:S(2)}) %collective-permute-start.26) | collective-permute-done | bytes 589856 | tf_op jit(solution)/shard_map/ppermute | solution.py:93
  209.5 12.1 %collective-permute-done.27 = bf16[1408,512]{1,0:T(8,128)(2,1)S(1)} collective-permute-done((bf16[1408,512]{1,0:T(8,128)(2,1)}, bf16[1408,512]{1,0:T(8,128)(2,1)S(1)}, u32[]{:S(2)}, u32[]{:S(2)}) %collective-permute-start.27) | collective-permute-done | bytes 1441824 | tf_op jit(solution)/shard_map/ppermute | solution.py:93
  227.4 15.1 %collective-permute-done.31 = bf16[288,1024]{1,0:T(8,128)(2,1)S(1)} collective-permute-done((bf16[288,1024]{1,0:T(8,128)(2,1)S(1)}, bf16[288,1024]{1,0:T(8,128)(2,1)S(1)}, u32[]{:S(2)}, u32[]{:S(2)}) %collective-permute-start.31) | collective-permute-done | bytes 589856 | tf_op jit(solution)/shard_map/ppermute | solution.py:93
  242.5 24.2 %collective-permute-done.34 = bf16[1408,512]{1,0:T(8,128)(2,1)S(1)} collective-permute-done((bf16[1408,512]{1,0:T(8,128)(2,1)S(1)}, bf16[1408,512]{1,0:T(8,128)(2,1)S(1)}, u32[]{:S(2)}, u32[]{:S(2)}) %collective-permute-start.34) | collective-permute-done | bytes 1441824 | tf_op jit(solution)/shard_map/ppermute | solution.py:93
  282.9 22.1 %collective-permute-done.35 = bf16[1408,512]{1,0:T(8,128)(2,1)S(1)} collective-permute-done((bf16[1408,512]{1,0:T(8,128)(2,1)S(1)}, bf16[1408,512]{1,0:T(8,128)(2,1)S(1)}, u32[]{:S(2)}, u32[]{:S(2)}) %collective-permute-start.35) | collective-permute-done | bytes 1441824 | tf_op jit(solution)/shard_map/ppermute | solution.py:93
  323.0 25.3 %collective-permute-done.39 = bf16[1408,512]{1,0:T(8,128)(2,1)S(1)} collective-permute-done((bf16[1408,512]{1,0:T(8,128)(2,1)}, bf16[1408,512]{1,0:T(8,128)(2,1)S(1)}, u32[]{:S(2)}, u32[]{:S(2)}) %collective-permute-start.39) | collective-permute-done | bytes 1441824 | tf_op jit(solution)/shard_map/ppermute | solution.py:93
  353.4 30.3 %collective-permute-done.43.refs_0_ = bf16[1408,512]{1,0:T(8,128)(2,1)} collective-permute-done((bf16[1408,512]{1,0:T(8,128)(2,1)S(1)}, bf16[1408,512]{1,0:T(8,128)(2,1)}, u32[]{:S(2)}, u32[]{:S(2)}) %collective-permute-start.43) | collective-permute-done | bytes 1441824 | tf_op jit(solution)/shard_map/ppermute | solution.py:93
  386.7 19.3 %shard_map.55.refs_4_ = f32[3,704,5632]{2,1,0:T(8,128)} custom-call(s32[1]{0:T(128)} %bitcast.3.place, bf16[3,704,2048]{2,1,0:T(8,128)(2,1)} %pad_maximum_fusion.scaled, bf16[1408,512]{1,0:T(8,128)(2,1)} %copy-done.10, bf16[1408,512]{1,0:T(8,128)(2,1)} %copy-done.20, bf16[1408,512]{1,0:T(8,128)(2,1)} %copy-done.13, bf16[1408,512]{1,0:T(8,128)(2,1)} %copy-done.23), custom_call_target="tpu_custom_call" | custom-call | flops 12180258816 | bytes 26312704 | tf_op jit(solution)/shard_map/pallas_call | solution.py:60
  412.3 31.2 %collective-permute-done.50.refs_2_ = bf16[1408,512]{1,0:T(8,128)(2,1)} collective-permute-done((bf16[1408,512]{1,0:T(8,128)(2,1)}, bf16[1408,512]{1,0:T(8,128)(2,1)}, u32[]{:S(2)}, u32[]{:S(2)}) %collective-permute-start.50) | collective-permute-done | bytes 1441824 | tf_op jit(solution)/shard_map/ppermute | solution.py:93
  445.6 19.2 %shard_map.56.refs_4_ = f32[3,704,5632]{2,1,0:T(8,128)} custom-call(s32[1]{0:T(128)} %bitcast.2.place, bf16[3,704,2048]{2,1,0:T(8,128)(2,1)} %pad_maximum_fusion.scaled, bf16[1408,512]{1,0:T(8,128)(2,1)} %collective-permute-done.36.refs_0_, bf16[1408,512]{1,0:T(8,128)(2,1)} %copy-done.22, ...), custom_call_target="tpu_custom_call", output_to_operand_aliasing={{}: (6, {})} | custom-call | flops 12180258816 | bytes 26312704 | tf_op jit(solution)/shard_map/pallas_call | solution.py:60
  479.4 19.1 %shard_map.57.refs_4_ = f32[3,704,5632]{2,1,0:T(8,128)} custom-call(s32[1]{0:T(128)} %bitcast.1.place, bf16[3,704,2048]{2,1,0:T(8,128)(2,1)} %pad_maximum_fusion.scaled, bf16[1408,512]{1,0:T(8,128)(2,1)} %copy-done.11, bf16[1408,512]{1,0:T(8,128)(2,1)} %copy-done.21, bf16[1408,512]{1,0:T(8,128)(2,1)} %get-tuple-element.435.refs_2_, ...), custom_call_target="tpu_custom_call", output_to_operand_aliasing={{}: (6, {})} | custom-call | flops 12180258816 | bytes 26312704 | tf_op jit(solution)/shard_map/pallas_call | solution.py:60
  510.1 19.2 %shard_map.58.refs_4_ = f32[3,704,5632]{2,1,0:T(8,128)} custom-call(s32[1]{0:T(128)} %bitcast.place, bf16[3,704,2048]{2,1,0:T(8,128)(2,1)} %pad_maximum_fusion.scaled, bf16[1408,512]{1,0:T(8,128)(2,1)} %collective-permute-done.43.refs_0_, bf16[1408,512]{1,0:T(8,128)(2,1)} %collective-permute-done.52.refs_1_, ...), custom_call_target="tpu_custom_call", output_to_operand_aliasing={{}: (6, {})} | custom-call | flops 12180258816 | bytes 26312704 | tf_op jit(solution)/shard_map/pallas_call | solution.py:60
  529.3 11.3 %collective-permute-done.60.refs_2_ = bf16[1408,512]{1,0:T(8,128)(2,1)} collective-permute-done((bf16[1408,512]{1,0:T(8,128)(2,1)}, bf16[1408,512]{1,0:T(8,128)(2,1)}, u32[]{:S(2)}, u32[]{:S(2)}) %collective-permute-start.60) | collective-permute-done | bytes 1441824 | tf_op jit(solution)/shard_map/ppermute | solution.py:93
  540.7 29.5 %collective-permute-done.63 = bf16[1408,512]{1,0:T(8,128)(2,1)S(1)} collective-permute-done((bf16[1408,512]{1,0:T(8,128)(2,1)}, bf16[1408,512]{1,0:T(8,128)(2,1)S(1)}, u32[]{:S(2)}, u32[]{:S(2)}) %collective-permute-start.63) | collective-permute-done | bytes 1441824 | tf_op jit(solution)/shard_map/ppermute | solution.py:93
  573.6 20.3 %shard_map.59.refs_4_ = f32[3,704,5632]{2,1,0:T(8,128)} custom-call(s32[1]{0:T(128)} %bitcast.3.place, bf16[3,704,2048]{2,1,0:T(8,128)(2,1)} %pad_maximum_fusion.1.scaled, bf16[1408,512]{1,0:T(8,128)(2,1)} %copy-done.12, bf16[1408,512]{1,0:T(8,128)(2,1)} %collective-permute-done.57.refs_1_, ...), custom_call_target="tpu_custom_call", output_to_operand_aliasing={{}: (6, {})} | custom-call | flops 12180258816 | bytes 38207488 | tf_op jit(solution)/shard_map/pallas_call | solution.py:60
  609.2 20.3 %shard_map.60.refs_4_ = f32[3,704,5632]{2,1,0:T(8,128)} custom-call(s32[1]{0:T(128)} %bitcast.2.place, bf16[3,704,2048]{2,1,0:T(8,128)(2,1)} %pad_maximum_fusion.1.scaled, bf16[1408,512]{1,0:T(8,128)(2,1)} %collective-permute-done.56.refs_0_, bf16[1408,512]{1,0:T(8,128)(2,1)} %collective-permute-done.62.refs_1_, ...), custom_call_target="tpu_custom_call", output_to_operand_aliasing={{}: (6, {})} | custom-call | flops 12180258816 | bytes 38207488 | tf_op jit(solution)/shard_map/pallas_call | solution.py:60
  629.5 10.8 %collective-permute-done.68.refs_2_ = bf16[1408,512]{1,0:T(8,128)(2,1)S(1)} collective-permute-done((bf16[1408,512]{1,0:T(8,128)(2,1)S(1)}, bf16[1408,512]{1,0:T(8,128)(2,1)S(1)}, u32[]{:S(2)}, u32[]{:S(2)}) %collective-permute-start.68) | collective-permute-done | bytes 1441824 | tf_op jit(solution)/shard_map/ppermute | solution.py:93
  641.5 20.6 %shard_map.61.refs_4_ = f32[3,704,5632]{2,1,0:T(8,128)} custom-call(s32[1]{0:T(128)} %bitcast.1.place, bf16[3,704,2048]{2,1,0:T(8,128)(2,1)} %pad_maximum_fusion.1.scaled, bf16[1408,512]{1,0:T(8,128)(2,1)} %copy-done.14, bf16[1408,512]{1,0:T(8,128)(2,1)} %copy-done.25, bf16[1408,512]{1,0:T(8,128)(2,1)} %copy-done.15, ...), custom_call_target="tpu_custom_call", output_to_operand_aliasing={{}: (6, {})} | custom-call | flops 12180258816 | bytes 38207488 | tf_op jit(solution)/shard_map/pallas_call | solution.py:60
  663.2 20.3 %shard_map.62 = f32[3,704,5632]{2,1,0:T(8,128)} custom-call(s32[1]{0:T(128)} %bitcast.place, bf16[3,704,2048]{2,1,0:T(8,128)(2,1)} %pad_maximum_fusion.1.scaled, bf16[1408,512]{1,0:T(8,128)(2,1)} %copy-done.24, bf16[1408,512]{1,0:T(8,128)(2,1)} %copy-done.27, bf16[1408,512]{1,0:T(8,128)(2,1)} %copy-done.26, ...), custom_call_target="tpu_custom_call", output_to_operand_aliasing={{}: (6, {})} | custom-call | flops 12180258816 | bytes 38207488 | tf_op jit(solution)/shard_map/pallas_call | solution.py:60
  (281 shorter events, 229.7 us)
Async XLA Ops:
  188.2 33.4 %collective-permute-start.27 = (bf16[1408,512]{1,0:T(8,128)(2,1)}, bf16[1408,512]{1,0:T(8,128)(2,1)S(1)}, u32[]{:S(2)}, u32[]{:S(2)}) collective-permute-start(bf16[1408,512]{1,0:T(8,128)(2,1)} %convolution_convert_fusion.1), channel_id=1, source_target_pairs={{0,1},{1,0},{2,3},{3,2},{4,5},{5,4},{6,7},{7,6},{8,9},{9,8},{10,11... | collective-permute-start | bytes 4325384 | tf_op jit(solution)/shard_map/ppermute | solution.py:93
  224.0 42.7 %collective-permute-start.34 = (bf16[1408,512]{1,0:T(8,128)(2,1)S(1)}, bf16[1408,512]{1,0:T(8,128)(2,1)S(1)}, u32[]{:S(2)}, u32[]{:S(2)}) collective-permute-start(bf16[1408,512]{1,0:T(8,128)(2,1)S(1)} %broadcast_select_fusion.6), channel_id=1, source_target_pairs={{8,16},{9,1},{10,18},{11,3},{12,20},{13,5},{14,22},{15,7},{16,24},... | collective-permute-start | bytes 4325384 | tf_op jit(solution)/shard_map/ppermute | solution.py:93
  267.1 38.0 %collective-permute-start.36 = (bf16[1408,512]{1,0:T(8,128)(2,1)S(1)}, bf16[1408,512]{1,0:T(8,128)(2,1)}, u32[]{:S(2)}, u32[]{:S(2)}) collective-permute-start(bf16[1408,512]{1,0:T(8,128)(2,1)S(1)} %get-tuple-element.411.refs_0_), channel_id=1, source_target_pairs={{0,4},{1,5},{2,6},{3,7},{4,0},{5,1},{6,2},{7,3},{8,12},{9,13},{10,... | collective-permute-start | bytes 4325384 | tf_op jit(solution)/shard_map/ppermute | solution.py:93
  267.7 37.4 %collective-permute-start.37 = (bf16[1408,512]{1,0:T(8,128)(2,1)S(1)}, bf16[1408,512]{1,0:T(8,128)(2,1)S(1)}, u32[]{:S(2)}, u32[]{:S(2)}) collective-permute-start(bf16[1408,512]{1,0:T(8,128)(2,1)S(1)} %get-tuple-element.411.refs_0_), channel_id=1, source_target_pairs={{0,2},{1,3},{2,0},{3,1},{4,6},{5,7},{6,4},{7,5},{8,10},{9,11},{10,... | collective-permute-start | bytes 4325384 | tf_op jit(solution)/shard_map/ppermute | solution.py:93
  267.7 37.4 %collective-permute-start.35 = (bf16[1408,512]{1,0:T(8,128)(2,1)S(1)}, bf16[1408,512]{1,0:T(8,128)(2,1)S(1)}, u32[]{:S(2)}, u32[]{:S(2)}) collective-permute-start(bf16[1408,512]{1,0:T(8,128)(2,1)S(1)} %get-tuple-element.518), channel_id=1, source_target_pairs={{8,16},{9,1},{10,18},{11,3},{12,20},{13,5},{14,22},{15,7},{16,24},... | collective-permute-start | bytes 4325384 | tf_op jit(solution)/shard_map/ppermute | solution.py:93
  307.2 41.1 %collective-permute-start.40 = (bf16[1408,512]{1,0:T(8,128)(2,1)S(1)}, bf16[1408,512]{1,0:T(8,128)(2,1)}, u32[]{:S(2)}, u32[]{:S(2)}) collective-permute-start(bf16[1408,512]{1,0:T(8,128)(2,1)S(1)} %get-tuple-element.413.refs_2_), channel_id=1, source_target_pairs={{0,4},{1,5},{2,6},{3,7},{4,0},{5,1},{6,2},{7,3},{8,12},{9,13},{10,... | collective-permute-start | bytes 4325384 | tf_op jit(solution)/shard_map/ppermute | solution.py:93
  308.7 39.6 %collective-permute-start.41 = (bf16[1408,512]{1,0:T(8,128)(2,1)S(1)}, bf16[1408,512]{1,0:T(8,128)(2,1)S(1)}, u32[]{:S(2)}, u32[]{:S(2)}) collective-permute-start(bf16[1408,512]{1,0:T(8,128)(2,1)S(1)} %get-tuple-element.413.refs_2_), channel_id=1, source_target_pairs={{0,2},{1,3},{2,0},{3,1},{4,6},{5,7},{6,4},{7,5},{8,10},{9,11},{10,... | collective-permute-start | bytes 4325384 | tf_op jit(solution)/shard_map/ppermute | solution.py:93
  312.4 35.9 %collective-permute-start.39 = (bf16[1408,512]{1,0:T(8,128)(2,1)}, bf16[1408,512]{1,0:T(8,128)(2,1)S(1)}, u32[]{:S(2)}, u32[]{:S(2)}) collective-permute-start(bf16[1408,512]{1,0:T(8,128)(2,1)} %get-tuple-element.516), channel_id=1, source_target_pairs={{8,16},{9,1},{10,18},{11,3},{12,20},{13,5},{14,22},{15,7},{16,24},... | collective-permute-start | bytes 4325384 | tf_op jit(solution)/shard_map/ppermute | solution.py:93
  313.8 34.5 %collective-permute-start.42 = (bf16[1408,512]{1,0:T(8,128)(2,1)}, bf16[1408,512]{1,0:T(8,128)(2,1)S(1)}, u32[]{:S(2)}, u32[]{:S(2)}) collective-permute-start(bf16[1408,512]{1,0:T(8,128)(2,1)} %collective-permute-done.36.refs_0_), channel_id=1, source_target_pairs={{0,2},{1,3},{2,0},{3,1},{4,6},{5,7},{6,4},{7,5},{8,10},{9,11},{10,... | collective-permute-start | bytes 4325384 | tf_op jit(solution)/shard_map/ppermute | solution.py:93
  350.8 32.9 %collective-permute-start.43 = (bf16[1408,512]{1,0:T(8,128)(2,1)S(1)}, bf16[1408,512]{1,0:T(8,128)(2,1)}, u32[]{:S(2)}, u32[]{:S(2)}) collective-permute-start(bf16[1408,512]{1,0:T(8,128)(2,1)S(1)} %get-tuple-element.433.refs_0_), channel_id=1, source_target_pairs={{0,4},{1,5},{2,6},{3,7},{4,0},{5,1},{6,2},{7,3},{8,12},{9,13},{10,... | collective-permute-start | bytes 4325384 | tf_op jit(solution)/shard_map/ppermute | solution.py:93
  351.6 54.3 %collective-permute-start.47 = (bf16[1408,512]{1,0:T(8,128)(2,1)S(1)}, bf16[1408,512]{1,0:T(8,128)(2,1)S(1)}, u32[]{:S(2)}, u32[]{:S(2)}) collective-permute-start(bf16[1408,512]{1,0:T(8,128)(2,1)S(1)} %convolution_convert_fusion), channel_id=1, source_target_pairs={{0,1},{1,0},{2,3},{3,2},{4,5},{5,4},{6,7},{7,6},{8,9},{9,8},{10,11... | collective-permute-start | bytes 4325384 | tf_op jit(solution)/shard_map/ppermute | solution.py:93
  351.6 54.3 %collective-permute-start.45 = (bf16[1408,512]{1,0:T(8,128)(2,1)}, bf16[1408,512]{1,0:T(8,128)(2,1)}, u32[]{:S(2)}, u32[]{:S(2)}) collective-permute-start(bf16[1408,512]{1,0:T(8,128)(2,1)} %collective-permute-done.40.refs_2_), channel_id=1, source_target_pairs={{0,2},{1,3},{2,0},{3,1},{4,6},{5,7},{6,4},{7,5},{8,10},{9,11},{10,... | collective-permute-start | bytes 4325384 | tf_op jit(solution)/shard_map/ppermute | solution.py:93
  352.2 53.8 %collective-permute-start.46 = (bf16[1408,512]{1,0:T(8,128)(2,1)}, bf16[1408,512]{1,0:T(8,128)(2,1)}, u32[]{:S(2)}, u32[]{:S(2)}) collective-permute-start(bf16[1408,512]{1,0:T(8,128)(2,1)} %get-tuple-element.513), channel_id=1, source_target_pairs={{8,16},{9,1},{10,18},{11,3},{12,20},{13,5},{14,22},{15,7},{16,24},... | collective-permute-start | bytes 4325384 | tf_op jit(solution)/shard_map/ppermute | solution.py:93
  409.2 34.3 %collective-permute-start.50 = (bf16[1408,512]{1,0:T(8,128)(2,1)}, bf16[1408,512]{1,0:T(8,128)(2,1)}, u32[]{:S(2)}, u32[]{:S(2)}) collective-permute-start(bf16[1408,512]{1,0:T(8,128)(2,1)} %get-tuple-element.435.refs_2_), channel_id=1, source_target_pairs={{0,4},{1,5},{2,6},{3,7},{4,0},{5,1},{6,2},{7,3},{8,12},{9,13},{10,... | collective-permute-start | bytes 4325384 | tf_op jit(solution)/shard_map/ppermute | solution.py:93
  410.3 54.5 %collective-permute-start.51 = (bf16[1408,512]{1,0:T(8,128)(2,1)}, bf16[1408,512]{1,0:T(8,128)(2,1)}, u32[]{:S(2)}, u32[]{:S(2)}) collective-permute-start(bf16[1408,512]{1,0:T(8,128)(2,1)} %get-tuple-element.435.refs_2_), channel_id=1, source_target_pairs={{0,2},{1,3},{2,0},{3,1},{4,6},{5,7},{6,4},{7,5},{8,10},{9,11},{10,... | collective-permute-start | bytes 4325384 | tf_op jit(solution)/shard_map/ppermute | solution.py:93
  410.5 54.3 %collective-permute-start.54 = (bf16[1408,512]{1,0:T(8,128)(2,1)S(1)}, bf16[1408,512]{1,0:T(8,128)(2,1)}, u32[]{:S(2)}, u32[]{:S(2)}) collective-permute-start(bf16[1408,512]{1,0:T(8,128)(2,1)S(1)} %collective-permute-done.47), channel_id=1, source_target_pairs={{0,2},{1,3},{2,0},{3,1},{4,6},{5,7},{6,4},{7,5},{8,10},{9,11},{10,... | collective-permute-start | bytes 4325384 | tf_op jit(solution)/shard_map/ppermute | solution.py:93
  410.8 54.0 %collective-permute-start.52 = (bf16[1408,512]{1,0:T(8,128)(2,1)}, bf16[1408,512]{1,0:T(8,128)(2,1)}, u32[]{:S(2)}, u32[]{:S(2)}) collective-permute-start(bf16[1408,512]{1,0:T(8,128)(2,1)} %collective-permute-done.43.refs_0_), channel_id=1, source_target_pairs={{0,2},{1,3},{2,0},{3,1},{4,6},{5,7},{6,4},{7,5},{8,10},{9,11},{10,... | collective-permute-start | bytes 4325384 | tf_op jit(solution)/shard_map/ppermute | solution.py:93
  411.0 53.8 %collective-permute-start.53 = (bf16[1408,512]{1,0:T(8,128)(2,1)}, bf16[1408,512]{1,0:T(8,128)(2,1)}, u32[]{:S(2)}, u32[]{:S(2)}) collective-permute-start(bf16[1408,512]{1,0:T(8,128)(2,1)} %get-tuple-element.511), channel_id=1, source_target_pairs={{8,16},{9,1},{10,18},{11,3},{12,20},{13,5},{14,22},{15,7},{16,24},... | collective-permute-start | bytes 4325384 | tf_op jit(solution)/shard_map/ppermute | solution.py:93
  467.6 33.3 %collective-permute-start.56 = (bf16[1408,512]{1,0:T(8,128)(2,1)S(1)}, bf16[1408,512]{1,0:T(8,128)(2,1)}, u32[]{:S(2)}, u32[]{:S(2)}) collective-permute-start(bf16[1408,512]{1,0:T(8,128)(2,1)S(1)} %get-tuple-element.464.refs_0_), channel_id=1, source_target_pairs={{0,4},{1,5},{2,6},{3,7},{4,0},{5,1},{6,2},{7,3},{8,12},{9,13},{10,... | collective-permute-start | bytes 4325384 | tf_op jit(solution)/shard_map/ppermute | solution.py:93
  469.4 36.0 %collective-permute-start.59 = (bf16[1408,512]{1,0:T(8,128)(2,1)}, bf16[1408,512]{1,0:T(8,128)(2,1)S(1)}, u32[]{:S(2)}, u32[]{:S(2)}) collective-permute-start(bf16[1408,512]{1,0:T(8,128)(2,1)} %get-tuple-element.509), channel_id=1, source_target_pairs={{8,16},{9,1},{10,18},{11,3},{12,20},{13,5},{14,22},{15,7},{16,24},... | collective-permute-start | bytes 4325384 | tf_op jit(solution)/shard_map/ppermute | solution.py:93
  507.3 33.3 %collective-permute-start.60 = (bf16[1408,512]{1,0:T(8,128)(2,1)}, bf16[1408,512]{1,0:T(8,128)(2,1)}, u32[]{:S(2)}, u32[]{:S(2)}) collective-permute-start(bf16[1408,512]{1,0:T(8,128)(2,1)} %get-tuple-element.466.refs_2_), channel_id=1, source_target_pairs={{0,4},{1,5},{2,6},{3,7},{4,0},{5,1},{6,2},{7,3},{8,12},{9,13},{10,... | collective-permute-start | bytes 4325384 | tf_op jit(solution)/shard_map/ppermute | solution.py:93
  508.8 61.4 %collective-permute-start.63 = (bf16[1408,512]{1,0:T(8,128)(2,1)}, bf16[1408,512]{1,0:T(8,128)(2,1)S(1)}, u32[]{:S(2)}, u32[]{:S(2)}) collective-permute-start(bf16[1408,512]{1,0:T(8,128)(2,1)} %get-tuple-element.507), channel_id=1, source_target_pairs={{8,16},{9,1},{10,18},{11,3},{12,20},{13,5},{14,22},{15,7},{16,24},... | collective-permute-start | bytes 4325384 | tf_op jit(solution)/shard_map/ppermute | solution.py:93
  570.4 33.0 %collective-permute-start.64 = (bf16[1408,512]{1,0:T(8,128)(2,1)S(1)}, bf16[1408,512]{1,0:T(8,128)(2,1)S(1)}, u32[]{:S(2)}, u32[]{:S(2)}) collective-permute-start(bf16[1408,512]{1,0:T(8,128)(2,1)S(1)} %select_select_fusion.1.refs_0_), channel_id=1, source_target_pairs={{0,4},{1,5},{2,6},{3,7},{4,0},{5,1},{6,2},{7,3},{8,12},{9,13},{10,... | collective-permute-start | bytes 4325384 | tf_op jit(solution)/shard_map/ppermute | solution.py:93
  572.0 35.4 %collective-permute-start.67 = (bf16[1408,512]{1,0:T(8,128)(2,1)S(1)}, bf16[1408,512]{1,0:T(8,128)(2,1)S(1)}, u32[]{:S(2)}, u32[]{:S(2)}) collective-permute-start(bf16[1408,512]{1,0:T(8,128)(2,1)S(1)} %collective-permute-done.63), channel_id=1, source_target_pairs={{9,1},{11,3},{13,5},{15,7},{16,24},{18,26},{20,28},{22,30}} | collective-permute-start | bytes 4325384 | tf_op jit(solution)/shard_map/ppermute | solution.py:93
  (86 other events, 1501.3 us)

commit v2 on v1

--- a/solution.py
+++ b/solution.py
@@ -9,7 +9,7 @@
 
 AXES = ("row", "col")
 BF16, F32 = jnp.bfloat16, jnp.float32
-SLAB_PARTS = 5
+SLAB_PARTS = 3
 PARTS = 2
 
 
@@ -30,8 +30,70 @@
     return lax.dot_general(scaled, partner, (((2,), (1,)), ((), ())), preferred_element_type=F32)
 
 
-def block_kernel(place, scaled, *refs, first):
-    pieces, out = refs[:4], refs[-1]
+def transform_kernel(at, *refs, counts, n_coef):
+    n_slab = sum(counts)
+    slabs, coefs = refs[:n_slab], refs[n_slab : n_slab + n_coef]
+    out, slab_v, coef_v, sems = refs[n_slab + n_coef :]
+    rows, width = coefs[0].shape[0], coef_v.shape[1]
+    copies = []
+    for i, piece in enumerate(coefs):
+        first = pl.multiple_of(at[len(counts) + i], 16)
+        column = pl.multiple_of(at[len(counts) + n_coef + i], 128)
+        copies.append(
+            pltpu.make_async_copy(
+                piece.at[:, pl.ds(column, width)], coef_v.at[pl.ds(first, rows)], sems.at[n_slab + i]
+            )
+        )
+    groups, used = [], 0
+    for count in counts:
+        group, begin = [], 0
+        for piece in slabs[used : used + count]:
+            held = slab_v.at[len(groups), begin : begin + piece.shape[0]]
+            group.append(pltpu.make_async_copy(piece, held, sems.at[used + len(group)]))
+            begin += piece.shape[0]
+        used += count
+        groups.append(group)
+    for copy in copies + [c for group in groups for c in group]:
+        copy.start()
+    for copy in copies:
+        copy.wait()
+    for i, group in enumerate(groups):
+        for copy in group:
+            copy.wait()
+        first = pl.multiple_of(at[i], 16)
+        value = jnp.dot(slab_v[i], coef_v[...], preferred_element_type=F32)
+        out[pl.ds(first, slab_v.shape[1]), :] = value.astype(out.dtype)
+
+
+def transform(groups, group_rows, coefs, coef_rows, columns, width):
+    slabs = [piece for group in groups for piece in group]
+    rows = sum(piece.shape[0] for piece in groups[0])
+    depth, nao = len(coefs) * coefs[0].shape[0], slabs[0].shape[1]
+    at = jnp.stack([jnp.asarray(v, jnp.int32) for v in (*group_rows, *coef_rows, *columns)])
+    total = len(groups) * rows
+    return pl.pallas_call(
+        functools.partial(transform_kernel, counts=[len(g) for g in groups], n_coef=len(coefs)),
+        out_shape=jax.ShapeDtypeStruct((total, width), BF16),
+        grid_spec=pltpu.PrefetchScalarGridSpec(
+            num_scalar_prefetch=1,
+            grid=(1,),
+            in_specs=[pl.BlockSpec(memory_space=pl.ANY)] * (len(slabs) + len(coefs)),
+            out_specs=pl.BlockSpec((total, width), lambda i, a: (0, 0)),
+            scratch_shapes=[
+                pltpu.VMEM((len(groups), rows, nao), BF16),
+                pltpu.VMEM((depth, width), BF16),
+                pltpu.SemaphoreType.DMA((len(slabs) + len(coefs),)),
+            ],
+        ),
+        compiler_params=pltpu.CompilerParams(vmem_limit_bytes=56 * 2**20),
+        cost_estimate=pl.CostEstimate(
+            flops=2 * total * nao * width, bytes_accessed=2 * (total * nao + nao * width), transcendentals=0
+        ),
+    )(at, *slabs, *coefs)
+
+
+def block_kernel(place, scaled, *refs, n_pieces, first):
+    pieces, out = refs[:n_pieces], refs[-1]
     width = pieces[0].shape[1]
     total = None
     for i, piece in enumerate(pieces):
@@ -42,23 +104,24 @@
             preferred_element_type=F32,
         )
         total = term if total is None else total + term
-    out[0] = total if first else total + refs[4][0]
-
-
-def add_block(out, shape, place, scaled, pieces, first):
-    freqs, rows, depth = scaled.shape
+    out[0] = total if first else total + refs[n_pieces][0]
+
+
+def add_block(out, shape, place, scaled, pieces, part, first):
+    freqs, rows, _ = scaled.shape
     cols, width = pieces[0].shape
+    depth = width * len(pieces)
     tile = rows // 2
     block = pl.BlockSpec((1, tile, cols), lambda f, i, p: (f, i, p[0]))
-    in_specs = [pl.BlockSpec((1, tile, depth), lambda f, i, p: (f, i, 0))]
-    in_specs += [pl.BlockSpec((cols, width), lambda f, i, p: (0, 0))] * 4
+    in_specs = [pl.BlockSpec((1, tile, depth), lambda f, i, p: (f, i, part))]
+    in_specs += [pl.BlockSpec((cols, width), lambda f, i, p: (0, 0))] * len(pieces)
     operands, aliases = [place.reshape(1).astype(jnp.int32), scaled, *pieces], {}
     if out is not None:
         in_specs.append(pl.BlockSpec(memory_space=pl.ANY) if first else block)
+        aliases = {len(operands): 0}
         operands.append(out)
-        aliases = {6: 0}
     return pl.pallas_call(
-        functools.partial(block_kernel, first=first),
+        functools.partial(block_kernel, n_pieces=len(pieces), first=first),
         out_shape=jax.ShapeDtypeStruct(shape, F32),
         grid_spec=pltpu.PrefetchScalarGridSpec(
             num_scalar_prefetch=1, grid=(freqs, 2), in_specs=in_specs, out_specs=block
@@ -117,7 +180,7 @@
 
         return move(a, target)
 
-    slab_rows, nao = half_slab.shape
+    slab_rows = half_slab.shape[0]
     chip_rows = 4 * slab_rows
     rows = chip_rows // 2
     coef_rows, virt_x = coef.shape
@@ -134,11 +197,11 @@
         names = list(env)
         env.update(zip(names, lax.optimization_barrier([env[n] for n in names])))
 
-    def slot(c, n):
-        up = [None] + [env.get(f"up{c}{i}") for i in (1, 2, 3)]
-        down = [None] + [env.get(f"down{c}{i}") for i in (1, 2, 3)]
+    def slot(n):
+        up = [None] + [env.get(f"up{i}") for i in (1, 2, 3)]
+        down = [None] + [env.get(f"down{i}") for i in (1, 2, 3)]
         if n == 0:
-            return env[f"coef{c}"]
+            return env["coef"]
         if n == 1:
             return jnp.where(z == 0, down[1], up[1])
         if n == 2:
@@ -152,37 +215,40 @@
         jnp.where(z <= 1, 3, 0),
     )
 
-    def line(c, i):
-        before = (env[f"coef{c}"],) * 2 if i == 1 else (env[f"up{c}{i - 1}"], env[f"down{c}{i - 1}"])
-        return {f"up{c}{i}": z_up(before[0], i), f"down{c}{i}": z_down(before[1], i)}
-
-    def cross(c, n):
-        piece = slot(c, n)
-        return {f"slot{c}{n}": piece, f"cross{c}{n}": over_y(piece)}
-
-    def cores(c):
-        mine = jnp.zeros((8, coef_rows, both), BF16)
+    def line(i):
+        before = (env["coef"],) * 2 if i == 1 else (env[f"up{i - 1}"], env[f"down{i - 1}"])
+        return {f"up{i}": z_up(before[0], i), f"down{i}": z_down(before[1], i)}
+
+    def cross(n):
+        piece = env[f"slot{n}"] = slot(n)
+        return {f"cross{n}": over_y(piece), f"kslot{n}": over_k(piece)}
+
+    def cross_k(n):
+        return {f"kcross{n}": over_k(env[f"cross{n}"])}
+
+    cuts = [slab_rows * i // SLAB_PARTS // 16 * 16 for i in range(SLAB_PARTS)] + [slab_rows]
+
+    def slab_part(i):
+        return {f"slab_x{i}": over_x(env["slab"][cuts[i] : cuts[i + 1]])}
+
+    def slab_part_k(i):
+        return {f"slab_kx{i}": over_k(env[f"slab_x{i}"])}
+
+    def transformed(c):
+        groups = [[env["slab"]], [env["slab_k"]]]
+        groups += [[env[f"slab_{name}{i}"] for i in range(SLAB_PARTS)] for name in ("x", "kx")]
+        group_rows = [
+            (core * 2 + side) * slab_rows for side in (x, 1 - x) for core in (k, 1 - k)
+        ]
+        coefs, coef_at, columns = [], [], []
         for n in range(4):
-            mine = lax.dynamic_update_slice(mine, env.pop(f"slot{c}{n}")[None], (planes[n] * 2 + y, 0, 0))
-            mine = lax.dynamic_update_slice(mine, env.pop(f"cross{c}{n}")[None], (planes[n] * 2 + 1 - y, 0, 0))
-        theirs = over_k(lax.dynamic_slice(mine, (0, 0, (1 - k) * width), (8, coef_rows, width)))
-        return {f"keep{c}": lax.dynamic_slice(mine, (0, 0, k * width), (8, coef_rows, width)), f"theirs{c}": theirs}
-
-    def transformed(c):
-        keep, theirs = env.pop(f"keep{c}"), env.pop(f"theirs{c}")
-        whole = jnp.where(k == 0, jnp.stack([keep, theirs], 1), jnp.stack([theirs, keep], 1)).reshape(nao, width)
-        return {f"own{c}0": jnp.dot(env["slab"], whole, preferred_element_type=F32).astype(BF16)}
-
-    def chip_slab():
-        slab = jnp.zeros((4, slab_rows, nao), BF16)
-        for name, at in (
-            ("slab_o", k * 2 + x),
-            ("slab_k", (1 - k) * 2 + x),
-            ("slab_x", k * 2 + 1 - x),
-            ("slab_kx", (1 - k) * 2 + 1 - x),
-        ):
-            slab = lax.dynamic_update_slice(slab, env.pop(name)[None], (at, 0, 0))
-        return {"slab": slab.reshape(chip_rows, nao)}
+            for name, at_y in (("slot", y), ("cross", 1 - y)):
+                for prefix, core in (("", k), ("k", 1 - k)):
+                    whole = env.get(f"{prefix}{name}{n}")
+                    coefs.append(env[f"{prefix}{name}{n}_{c}"] if whole is None else whole)
+                    columns.append(k * width + (0 if whole is None else c * both))
+                    coef_at.append(((planes[n] * 2 + at_y) * 2 + core) * coef_rows)
+        return {f"own{c}0": transform(groups, group_rows, coefs, coef_at, columns, width)}
 
     def panel(c):
         parts = []
@@ -215,59 +281,59 @@
         held = jnp.where(u <= 1, item(t), jnp.where(u == 2, env[f"got{t}"], env[f"got{t + 1}"]))
         return {f"a{t}": held, f"b{t}": over_y(held), f"ka{t}": over_k(held)}
 
-    def take_k(t):
+    def taken(t):
         return {f"kb{t}": over_k(env[f"b{t}"])}
 
-    def block(t, crossed):
+    def block(t, crossed, pieces_of, part, first):
         c, near, _ = items[t]
         plane = jnp.where(u == 0, 1 - near, near)
         plane = jnp.where(x == 0, plane, 1 - plane)
         place = plane * 2 + (1 - y if crossed else y)
-        s = "b" if crossed else "a"
-        pieces = [env.pop(f"{h}{s}{i}") for i in (t, t + 1) for h in ("", "k")]
-        env["out"] = add_block(env.get("out"), shape, place, env[f"scaled{c}"], pieces, c == 0)
-
-    for c in range(PARTS):
-        env[f"coef{c}"] = coef[:, c * both : (c + 1) * both]
-    env["slab_o"] = half_slab
-    step()
-    cuts = [slab_rows * i // SLAB_PARTS // 16 * 16 for i in range(SLAB_PARTS)] + [slab_rows]
-
-    def slab_part(i):
-        return {f"slab_x{i}": over_x(env["slab_o"][cuts[i] : cuts[i + 1]])}
-
-    step(**line(0, 1), **cross(0, 0), **slab_part(0), slab_k=over_k(env["slab_o"]))
-    step(**line(0, 2), **cross(0, 1), **slab_part(1))
-    step(**line(0, 3), **cross(0, 2), **slab_part(2))
-    step(**line(1, 1), **cross(0, 3), **slab_part(3))
-    step(**line(1, 2), **cross(1, 0), **cores(0), **slab_part(4))
-    env["slab_x"] = jnp.concatenate([env.pop(f"slab_x{i}") for i in range(SLAB_PARTS)], 0)
-    step(**line(1, 3), **cross(1, 1), slab_kx=over_k(env["slab_x"]))
-    env.update(chip_slab())
+        env["out"] = add_block(env.get("out"), shape, place, env[f"scaled{c}"], pieces_of, part, first)
+
+    env["coef"], env["slab"] = coef, half_slab
+    step(**line(1), **cross(0), **slab_part(0), slab_k=over_k(env["slab"]))
+    step(**line(2), **cross(1), **slab_part(1), **slab_part_k(0), **cross_k(0))
+    step(**line(3), **cross(2), **slab_part(2), **slab_part_k(1), **cross_k(1))
+    env["slot3"] = slot(3)
+    halves = [env["slot3"][:, c * both : (c + 1) * both] for c in range(PARTS)]
+    env.update(later=halves[1])
+    step(cross3_0=over_y(halves[0]), kslot3=over_k(env["slot3"]), **slab_part_k(2), **cross_k(2))
+    env["kcross3_0"] = over_k(env["cross3_0"])
     step(**transformed(0))
-    step(**cross(1, 2), own01=over_x(env["own00"]), kown00=over_k(env["own00"]), **exchange(0, 0), **along(0))
-    step(**cross(1, 3), kown01=over_k(env["own01"]), **exchange(0, 1), **along(1))
-    step(**along(2), **take(0), **panel(0), **cores(1))
-    r = along(3) | take(1) | take_k(0)
-    env.update(transformed(1))
-    step(**r)
-    for t in range(2, count + 1):
-        r = take(t) if t < count else {}
-        r |= take_k(t - 1)
-        if t + 2 <= count:
-            r |= along(t + 2)
+
+    for t in range(count + 2):
+        r = along(t) if t <= count else {}
+        if t == 0:
+            r |= dict(cross3_1=over_y(env.pop("later")))
+            r |= dict(own01=over_x(env["own00"]), kown00=over_k(env["own00"])) | exchange(0, 0)
+        if t == 1:
+            env["kcross3_1"] = over_k(env["cross3_1"])
+            r |= dict(kown01=over_k(env["own01"])) | exchange(0, 1)
+            r |= transformed(1)
         if t == 2:
-            r |= dict(own11=over_x(env["own10"]), kown10=over_k(env["own10"])) | exchange(1, 0)
+            r |= panel(0) | exchange(1, 0)
+            r |= dict(own11=over_x(env["own10"]), kown10=over_k(env["own10"]))
         if t == 3:
             r |= dict(kown11=over_k(env["own11"])) | exchange(1, 1)
-        if t == 4:
+        if t == 5:
             r |= panel(1)
-        if t % 2 == 0:
-            block(t - 2, False)
-        elif t > 2:
-            block(t - 3, True)
+        if t >= 2:
+            r |= take(t - 2)
+        if t >= 3:
+            r |= taken(t - 3)
+        if t >= 3 and t % 2 == 1:
+            i = t - 3
+            pieces = [env.pop(f"a{i}"), env.pop(f"ka{i}"), r.pop(f"a{i + 1}"), r.pop(f"ka{i + 1}")]
+            block(i, False, pieces, 0, i < count // PARTS)
+        if t >= 4 and t % 2 == 0:
+            i = t - 4
+            pieces = [env.pop(f"b{i}"), env.pop(f"kb{i}"), env.pop(f"b{i + 1}"), r.pop(f"kb{i + 1}")]
+            block(i, True, pieces, 0, i < count // PARTS)
+        if t == count + 1:
+            block(count - 2, True, [env.pop(f"b{count - 2}"), r.pop(f"kb{count - 2}")], 0, False)
         step(**r)
-    block(count - 2, True)
+    block(count - 2, True, [env[f"b{count - 1}"], taken(count - 1)[f"kb{count - 1}"]], 1, False)
     return env["out"]
 
 

time: 694 us -> 582 us (0.84)
  waiting for transfers between devices: 333 us -> 262 us
  local copies, waits for them, and re-layouts: 60.3 us -> 18.2 us
  Pallas kernels: 158 us -> 194 us
  matrix products: 19.6 us -> 0 us
  starting transfers between devices: 67.4 us -> 57.9 us
    ppermute x72 -> x70, waiting for transfers between devices: 333 us -> 262 us  [move(): return lax.ppermute(array, AXES, pairs)]
    pallas_call x8 -> x11, Pallas kernels: 158 us -> 194 us  [the longest x9 168 us: add_block(): pl.pallas_call(functools.partial(block_kernel, n_pieces=len(pieces), firs...]
    dynamic_update_slice x20 -> x0, local copies, waits for them, and re-layouts: 26 us -> none  [the longest x4 13.5 us: chip_slab(): slab = lax.dynamic_update_slice(slab, env.pop(name)[None], (at, 0, 0))]
    dot_general x2 -> x0, matrix products: 19.6 us -> none  [transformed(): jnp.dot(env['slab'], whole, preferred_element_type=F32).astype(BF16)]
    ppermute x72 -> x70, starting transfers between devices: 67.4 us -> 57.9 us  [move(): return lax.ppermute(array, AXES, pairs)]
  transfers between devices with their start and end apart: 72 -> 70, of which waited for: 30 -> 28; matrix products, arithmetic and copies ran while one was open for 8% -> 6% of each run, Pallas kernels for 20% -> 29%
where the time goes in v2:
time: 582 us; the launch traced here: 574 us
  waiting for transfers between devices  262 us (45%)
  Pallas kernels  194 us (33%)
  starting transfers between devices  57.9 us (10%)
  other arithmetic  39.8 us (7%)
  local copies, waits for them, and re-layouts  18.2 us (3%)
    ppermute x70, waiting for transfers between devices, move(): return lax.ppermute(array, AXES, pairs)  262 us
    pallas_call x9, Pallas kernels, add_block(): pl.pallas_call(functools.partial(block_kernel, n_pieces=len(pieces), firs...  168 us
    ppermute x70, starting transfers between devices, move(): return lax.ppermute(array, AXES, pairs)  57.9 us
    pallas_call x2, Pallas kernels, transform(): pl.pallas_call(functools.partial(transform_kernel, counts=[len(g) for g i...  25.7 us
  transfers between devices with their start and end apart: 70, of which 28 were waited for; matrix products, arithmetic and copies ran while one was open for 6% of the time, Pallas kernels for 29%

profile of v2, /device:TPU:2, one launch (start us, length us, event | category | flops | bytes accessed | tf_op | source)
XLA Modules:
  0.0 573.9 jit_solution(7027855400460713876)
XLA Ops:
  9.4 17.3 %collective-permute-done.4.refs_2_ = bf16[112,4608]{1,0:T(8,128)(2,1)} collective-permute-done((bf16[112,4608]{1,0:T(8,128)(2,1)S(1)}, bf16[112,4608]{1,0:T(8,128)(2,1)}, u32[]{:S(2)}, u32[]{:S(2)}) %collective-permute-start.4) | collective-permute-done | bytes 1032224 | tf_op jit(solution)/shard_map/ppermute | solution.py:156
  47.1 16.6 %collective-permute-done.10.refs_3_ = bf16[112,4608]{1,0:T(8,128)(2,1)} collective-permute-done((bf16[112,4608]{1,0:T(8,128)(2,1)}, bf16[112,4608]{1,0:T(8,128)(2,1)}, u32[]{:S(2)}, u32[]{:S(2)}) %collective-permute-start.10) | collective-permute-done | bytes 1032224 | tf_op jit(solution)/shard_map/ppermute | solution.py:156
  85.6 23.3 %collective-permute-done.14 = bf16[288,2048]{1,0:T(8,128)(2,1)} collective-permute-done((bf16[288,2048]{1,0:T(8,128)(2,1)}, bf16[288,2048]{1,0:T(8,128)(2,1)}, u32[]{:S(2)}, u32[]{:S(2)}) %collective-permute-start.14) | collective-permute-done | bytes 1179680 | tf_op jit(solution)/shard_map/ppermute | solution.py:156
  117.4 15.3 %collective-permute-done.20.refs_22_ = bf16[288,1024]{1,0:T(8,128)(2,1)} collective-permute-done((bf16[288,1024]{1,0:T(8,128)(2,1)S(1)}, bf16[288,1024]{1,0:T(8,128)(2,1)}, u32[]{:S(2)}, u32[]{:S(2)}) %collective-permute-start.20) | collective-permute-done | bytes 589856 | tf_op jit(solution)/shard_map/ppermute | solution.py:156
  135.2 12.8 %shard_map.55 = bf16[1408,512]{1,0:T(8,128)(2,1)} custom-call(s32[36]{0:T(128)} %stack.69.at, bf16[352,4608]{1,0:T(8,128)(2,1)} %refs_0_.1, bf16[352,4608]{1,0:T(8,128)(2,1)} %collective-permute-done.5.refs_1_, bf16[112,4608]{1,0:T(8,128)(2,1)} %collective-permute-done.4.refs_2_, bf16[112,4608]{1,0:T(8,128)(2,1)} %collective-permute-done.10.refs_3_, ...), custom_call_target="tpu_custom_call" | custom-call | flops 6643777536 | bytes 17694720 | tf_op jit(solution)/shard_map/pallas_call | solution.py:74
  151.7 15.4 %collective-permute-done.26.refs_22_ = bf16[288,1024]{1,0:T(8,128)(2,1)S(1)} collective-permute-done((bf16[288,1024]{1,0:T(8,128)(2,1)}, bf16[288,1024]{1,0:T(8,128)(2,1)S(1)}, u32[]{:S(2)}, u32[]{:S(2)}) %collective-permute-start.26) | collective-permute-done | bytes 589856 | tf_op jit(solution)/shard_map/ppermute | solution.py:156
  167.1 16.5 %collective-permute-done.27 = bf16[1408,512]{1,0:T(8,128)(2,1)S(1)} collective-permute-done((bf16[1408,512]{1,0:T(8,128)(2,1)}, bf16[1408,512]{1,0:T(8,128)(2,1)S(1)}, u32[]{:S(2)}, u32[]{:S(2)}) %collective-permute-start.27) | collective-permute-done | bytes 1441824 | tf_op jit(solution)/shard_map/ppermute | solution.py:156
  193.6 12.9 %shard_map.56 = bf16[1408,512]{1,0:T(8,128)(2,1)} custom-call(s32[36]{0:T(128)} %stack.71.at, bf16[352,4608]{1,0:T(8,128)(2,1)} %refs_0_.1, bf16[352,4608]{1,0:T(8,128)(2,1)} %collective-permute-done.5.refs_1_, bf16[112,4608]{1,0:T(8,128)(2,1)} %collective-permute-done.4.refs_2_, bf16[112,4608]{1,0:T(8,128)(2,1)} %collective-permute-done.10.refs_3_, ...), custom_call_target="tpu_custom_call" | custom-call | flops 6643777536 | bytes 17694720 | tf_op jit(solution)/shard_map/pallas_call | solution.py:74
  206.5 19.7 %collective-permute-done.31 = bf16[1408,512]{1,0:T(8,128)(2,1)} collective-permute-done((bf16[1408,512]{1,0:T(8,128)(2,1)}, bf16[1408,512]{1,0:T(8,128)(2,1)}, u32[]{:S(2)}, u32[]{:S(2)}) %collective-permute-start.31) | collective-permute-done | bytes 1441824 | tf_op jit(solution)/shard_map/ppermute | solution.py:156
  241.8 20.3 %collective-permute-done.34 = bf16[1408,512]{1,0:T(8,128)(2,1)S(1)} collective-permute-done((bf16[1408,512]{1,0:T(8,128)(2,1)S(1)}, bf16[1408,512]{1,0:T(8,128)(2,1)S(1)}, u32[]{:S(2)}, u32[]{:S(2)}) %collective-permute-start.34) | collective-permute-done | bytes 1441824 | tf_op jit(solution)/shard_map/ppermute | solution.py:156
  280.0 19.3 %shard_map.57.refs_4_ = f32[3,704,5632]{2,1,0:T(8,128)} custom-call(s32[1]{0:T(128)} %bitcast.24.place, bf16[3,704,2048]{2,1,0:T(8,128)(2,1)} %pad_maximum_fusion.scaled, bf16[1408,512]{1,0:T(8,128)(2,1)} %copy-done.17, bf16[1408,512]{1,0:T(8,128)(2,1)} %copy-done.30, bf16[1408,512]{1,0:T(8,128)(2,1)} %get-tuple-element.442.refs_2_, ...), custom_call_target="tpu_custom_call" | custom-call | flops 12180258816 | bytes 26312704 | tf_op jit(solution)/shard_map/pallas_call | solution.py:123
  299.3 16.7 %collective-permute-done.41 = bf16[1408,512]{1,0:T(8,128)(2,1)} collective-permute-done((bf16[1408,512]{1,0:T(8,128)(2,1)}, bf16[1408,512]{1,0:T(8,128)(2,1)}, u32[]{:S(2)}, u32[]{:S(2)}) %collective-permute-start.41) | collective-permute-done | bytes 1441824 | tf_op jit(solution)/shard_map/ppermute | solution.py:156
  321.7 19.1 %shard_map.58.refs_4_ = f32[3,704,5632]{2,1,0:T(8,128)} custom-call(s32[1]{0:T(128)} %bitcast.25.place, bf16[3,704,2048]{2,1,0:T(8,128)(2,1)} %pad_maximum_fusion.scaled, bf16[1408,512]{1,0:T(8,128)(2,1)} %collective-permute-done.38.refs_0_, bf16[1408,512]{1,0:T(8,128)(2,1)} %collective-permute-done.45.refs_1_, ...), custom_call_target="tpu_custom_call", output_to_operand_aliasing={{}: (6, {})} | custom-call | flops 12180258816 | bytes 26312704 | tf_op jit(solution)/shard_map/pallas_call | solution.py:123
  340.9 14.8 %collective-permute-done.47 = bf16[1408,512]{1,0:T(8,128)(2,1)} collective-permute-done((bf16[1408,512]{1,0:T(8,128)(2,1)}, bf16[1408,512]{1,0:T(8,128)(2,1)}, u32[]{:S(2)}, u32[]{:S(2)}) %collective-permute-start.47) | collective-permute-done | bytes 1441824 | tf_op jit(solution)/shard_map/ppermute | solution.py:156
  370.0 19.2 %shard_map.59.refs_4_ = f32[3,704,5632]{2,1,0:T(8,128)} custom-call(s32[1]{0:T(128)} %bitcast.26.place, bf16[3,704,2048]{2,1,0:T(8,128)(2,1)} %pad_maximum_fusion.scaled, bf16[1408,512]{1,0:T(8,128)(2,1)} %get-tuple-element.382.refs_0_, bf16[1408,512]{1,0:T(8,128)(2,1)} %collective-permute-done.49.refs_1_, ...), custom_call_target="tpu_custom_call", output_to_operand_aliasing={{}: (6, {})} | custom-call | flops 12180258816 | bytes 26312704 | tf_op jit(solution)/shard_map/pallas_call | solution.py:123
  401.4 19.3 %shard_map.60.refs_4_ = f32[3,704,5632]{2,1,0:T(8,128)} custom-call(s32[1]{0:T(128)} %bitcast.place, bf16[3,704,2048]{2,1,0:T(8,128)(2,1)} %pad_maximum_fusion.scaled, bf16[1408,512]{1,0:T(8,128)(2,1)} %collective-permute-done.48.refs_0_, bf16[1408,512]{1,0:T(8,128)(2,1)} %collective-permute-done.53.refs_1_, ...), custom_call_target="tpu_custom_call", output_to_operand_aliasing={{}: (6, {})} | custom-call | flops 12180258816 | bytes 26312704 | tf_op jit(solution)/shard_map/pallas_call | solution.py:123
  420.7 15.9 %collective-permute-done.55 = bf16[1408,512]{1,0:T(8,128)(2,1)S(1)} collective-permute-done((bf16[1408,512]{1,0:T(8,128)(2,1)}, bf16[1408,512]{1,0:T(8,128)(2,1)S(1)}, u32[]{:S(2)}, u32[]{:S(2)}) %collective-permute-start.55) | collective-permute-done | bytes 1441824 | tf_op jit(solution)/shard_map/ppermute | solution.py:156
  441.3 20.3 %shard_map.61.refs_4_ = f32[3,704,5632]{2,1,0:T(8,128)} custom-call(s32[1]{0:T(128)} %bitcast.24.place, bf16[3,704,2048]{2,1,0:T(8,128)(2,1)} %pad_maximum_fusion.1.scaled, bf16[1408,512]{1,0:T(8,128)(2,1)} %get-tuple-element.406.refs_0_, bf16[1408,512]{1,0:T(8,128)(2,1)} %collective-permute-done.57.refs_1_, ...), custom_call_target="tpu_custom_call", output_to_operand_aliasing={{}: (6, {})} | custom-call | flops 12180258816 | bytes 38207488 | tf_op jit(solution)/shard_map/pallas_call | solution.py:123
  461.6 14.0 %collective-permute-done.59 = bf16[1408,512]{1,0:T(8,128)(2,1)S(1)} collective-permute-done((bf16[1408,512]{1,0:T(8,128)(2,1)}, bf16[1408,512]{1,0:T(8,128)(2,1)S(1)}, u32[]{:S(2)}, u32[]{:S(2)}) %collective-permute-start.59) | collective-permute-done | bytes 1441824 | tf_op jit(solution)/shard_map/ppermute | solution.py:156
  480.3 20.4 %shard_map.62.refs_4_ = f32[3,704,5632]{2,1,0:T(8,128)} custom-call(s32[1]{0:T(128)} %bitcast.25.place, bf16[3,704,2048]{2,1,0:T(8,128)(2,1)} %pad_maximum_fusion.1.scaled, bf16[1408,512]{1,0:T(8,128)(2,1)} %collective-permute-done.56.refs_0_, bf16[1408,512]{1,0:T(8,128)(2,1)} %copy-done.32, ...), custom_call_target="tpu_custom_call", output_to_operand_aliasing={{}: (6, {})} | custom-call | flops 12180258816 | bytes 38207488 | tf_op jit(solution)/shard_map/pallas_call | solution.py:123
  500.7 12.1 %collective-permute-done.63 = bf16[1408,512]{1,0:T(8,128)(2,1)S(1)} collective-permute-done((bf16[1408,512]{1,0:T(8,128)(2,1)S(1)}, bf16[1408,512]{1,0:T(8,128)(2,1)S(1)}, u32[]{:S(2)}, u32[]{:S(2)}) %collective-permute-start.63) | collective-permute-done | bytes 1441824 | tf_op jit(solution)/shard_map/ppermute | solution.py:156
  517.4 20.3 %shard_map.63.refs_2_ = f32[3,704,5632]{2,1,0:T(8,128)} custom-call(s32[1]{0:T(128)} %bitcast.26.place, bf16[3,704,2048]{2,1,0:T(8,128)(2,1)} %pad_maximum_fusion.1.scaled, bf16[1408,512]{1,0:T(8,128)(2,1)} %copy-done.19, bf16[1408,512]{1,0:T(8,128)(2,1)} %collective-permute-done.65.refs_1_, ...), custom_call_target="tpu_custom_call", output_to_operand_aliasing={{}: (6, {})} | custom-call | flops 12180258816 | bytes 38207488 | tf_op jit(solution)/shard_map/pallas_call | solution.py:123
  538.8 15.1 %shard_map.64.refs_2_ = f32[3,704,5632]{2,1,0:T(8,128)} custom-call(s32[1]{0:T(128)} %bitcast.place, bf16[3,704,2048]{2,1,0:T(8,128)(2,1)} %pad_maximum_fusion.1.scaled, bf16[1408,512]{1,0:T(8,128)(2,1)} %copy-done.31, bf16[1408,512]{1,0:T(8,128)(2,1)} %copy-done.35, f32[3,704,5632]{2,1,0:T(8,128)} %shard_map.63.refs_2_), custom_call_target="tpu_custom_call", output_to_operand_aliasing={{}: (4, {})} | custom-call | flops 6090129408 | bytes 30998528 | tf_op jit(solution)/shard_map/pallas_call | solution.py:123
  558.3 15.1 %shard_map.65 = f32[3,704,5632]{2,1,0:T(8,128)} custom-call(s32[1]{0:T(128)} %bitcast.place, bf16[3,704,2048]{2,1,0:T(8,128)(2,1)} %pad_maximum_fusion.1.scaled, bf16[1408,512]{1,0:T(8,128)(2,1)} %copy-done.34, bf16[1408,512]{1,0:T(8,128)(2,1)} %copy-done.37, f32[3,704,5632]{2,1,0:T(8,128)} %shard_map.64.refs_2_), custom_call_target="tpu_custom_call", output_to_operand_aliasing={{}: (4, {})} | custom-call | flops 6090129408 | bytes 30998528 | tf_op jit(solution)/shard_map/pallas_call | solution.py:123
  (253 shorter events, 160.1 us)
Async XLA Ops:
  0.0 37.4 %collective-permute-start.5 = (bf16[352,4608]{1,0:T(8,128)(2,1)}, bf16[352,4608]{1,0:T(8,128)(2,1)}, u32[]{:S(2)}, u32[]{:S(2)}) collective-permute-start(bf16[352,4608]{1,0:T(8,128)(2,1)} %refs_0_.1), channel_id=1, source_target_pairs={{0,2},{1,3},{2,0},{3,1},{4,6},{5,7},{6,4},{7,5},{8,10},{9,11},{10,... | collective-permute-start | bytes 9732104 | tf_op jit(solution)/shard_map/ppermute | solution.py:156
  187.3 39.0 %collective-permute-start.31 = (bf16[1408,512]{1,0:T(8,128)(2,1)}, bf16[1408,512]{1,0:T(8,128)(2,1)}, u32[]{:S(2)}, u32[]{:S(2)}) collective-permute-start(bf16[1408,512]{1,0:T(8,128)(2,1)} %broadcast_select_fusion.6), channel_id=1, source_target_pairs={{8,16},{9,1},{10,18},{11,3},{12,20},{13,5},{14,22},{15,7},{16,24},... | collective-permute-start | bytes 4325384 | tf_op jit(solution)/shard_map/ppermute | solution.py:156
  188.5 37.7 %collective-permute-start.32 = (bf16[1408,512]{1,0:T(8,128)(2,1)S(1)}, bf16[1408,512]{1,0:T(8,128)(2,1)}, u32[]{:S(2)}, u32[]{:S(2)}) collective-permute-start(bf16[1408,512]{1,0:T(8,128)(2,1)S(1)} %collective-permute-done.27), channel_id=1, source_target_pairs={{0,2},{1,3},{2,0},{3,1},{4,6},{5,7},{6,4},{7,5},{8,10},{9,11},{10,... | collective-permute-start | bytes 4325384 | tf_op jit(solution)/shard_map/ppermute | solution.py:156
  188.6 37.6 %collective-permute-start.33 = (bf16[1408,512]{1,0:T(8,128)(2,1)S(1)}, bf16[1408,512]{1,0:T(8,128)(2,1)}, u32[]{:S(2)}, u32[]{:S(2)}) collective-permute-start(bf16[1408,512]{1,0:T(8,128)(2,1)S(1)} %collective-permute-done.27), channel_id=1, source_target_pairs={{0,8},{2,10},{4,12},{6,14},{8,0},{10,2},{12,4},{14,6},{17,25},{19,... | collective-permute-start | bytes 4325384 | tf_op jit(solution)/shard_map/ppermute | solution.py:156
  229.4 39.6 %collective-permute-start.35 = (bf16[1408,512]{1,0:T(8,128)(2,1)S(1)}, bf16[1408,512]{1,0:T(8,128)(2,1)S(1)}, u32[]{:S(2)}, u32[]{:S(2)}) collective-permute-start(bf16[1408,512]{1,0:T(8,128)(2,1)S(1)} %copy-done.1), channel_id=1, source_target_pairs={{0,8},{2,10},{4,12},{6,14},{8,0},{10,2},{12,4},{14,6},{17,25},{19,... | collective-permute-start | bytes 4325384 | tf_op jit(solution)/shard_map/ppermute | solution.py:156
  230.1 39.8 %collective-permute-start.36 = (bf16[1408,512]{1,0:T(8,128)(2,1)S(1)}, bf16[1408,512]{1,0:T(8,128)(2,1)S(1)}, u32[]{:S(2)}, u32[]{:S(2)}) collective-permute-start(bf16[1408,512]{1,0:T(8,128)(2,1)S(1)} %copy-done.1), channel_id=1, source_target_pairs={{0,1},{1,0},{2,3},{3,2},{4,5},{5,4},{6,7},{7,6},{8,9},{9,8},{10,11... | collective-permute-start | bytes 4325384 | tf_op jit(solution)/shard_map/ppermute | solution.py:156
  275.1 41.0 %collective-permute-start.42 = (bf16[1408,512]{1,0:T(8,128)(2,1)S(1)}, bf16[1408,512]{1,0:T(8,128)(2,1)}, u32[]{:S(2)}, u32[]{:S(2)}) collective-permute-start(bf16[1408,512]{1,0:T(8,128)(2,1)S(1)} %collective-permute-done.36), channel_id=1, source_target_pairs={{0,2},{1,3},{2,0},{3,1},{4,6},{5,7},{6,4},{7,5},{8,10},{9,11},{10,... | collective-permute-start | bytes 4325384 | tf_op jit(solution)/shard_map/ppermute | solution.py:156
  275.6 40.5 %collective-permute-start.43 = (bf16[1408,512]{1,0:T(8,128)(2,1)S(1)}, bf16[1408,512]{1,0:T(8,128)(2,1)}, u32[]{:S(2)}, u32[]{:S(2)}) collective-permute-start(bf16[1408,512]{1,0:T(8,128)(2,1)S(1)} %collective-permute-done.36), channel_id=1, source_target_pairs={{0,8},{2,10},{4,12},{6,14},{8,0},{10,2},{12,4},{14,6},{17,25},{19,... | collective-permute-start | bytes 4325384 | tf_op jit(solution)/shard_map/ppermute | solution.py:156
  277.3 38.7 %collective-permute-start.41 = (bf16[1408,512]{1,0:T(8,128)(2,1)}, bf16[1408,512]{1,0:T(8,128)(2,1)}, u32[]{:S(2)}, u32[]{:S(2)}) collective-permute-start(bf16[1408,512]{1,0:T(8,128)(2,1)} %get-tuple-element.441), channel_id=1, source_target_pairs={{8,16},{9,1},{10,18},{11,3},{12,20},{13,5},{14,22},{15,7},{16,24},... | collective-permute-start | bytes 4325384 | tf_op jit(solution)/shard_map/ppermute | solution.py:156
  278.6 37.4 %collective-permute-start.44 = (bf16[1408,512]{1,0:T(8,128)(2,1)}, bf16[1408,512]{1,0:T(8,128)(2,1)}, u32[]{:S(2)}, u32[]{:S(2)}) collective-permute-start(bf16[1408,512]{1,0:T(8,128)(2,1)} %get-tuple-element.442.refs_2_), channel_id=1, source_target_pairs={{0,4},{1,5},{2,6},{3,7},{4,0},{5,1},{6,2},{7,3},{8,12},{9,13},{10,... | collective-permute-start | bytes 4325384 | tf_op jit(solution)/shard_map/ppermute | solution.py:156
  279.9 36.2 %collective-permute-start.45 = (bf16[1408,512]{1,0:T(8,128)(2,1)}, bf16[1408,512]{1,0:T(8,128)(2,1)}, u32[]{:S(2)}, u32[]{:S(2)}) collective-permute-start(bf16[1408,512]{1,0:T(8,128)(2,1)} %collective-permute-done.38.refs_0_), channel_id=1, source_target_pairs={{0,2},{1,3},{2,0},{3,1},{4,6},{5,7},{6,4},{7,5},{8,10},{9,11},{10,... | collective-permute-start | bytes 4325384 | tf_op jit(solution)/shard_map/ppermute | solution.py:156
  319.4 36.2 %collective-permute-start.47 = (bf16[1408,512]{1,0:T(8,128)(2,1)}, bf16[1408,512]{1,0:T(8,128)(2,1)}, u32[]{:S(2)}, u32[]{:S(2)}) collective-permute-start(bf16[1408,512]{1,0:T(8,128)(2,1)} %get-tuple-element.440), channel_id=1, source_target_pairs={{8,16},{9,1},{10,18},{11,3},{12,20},{13,5},{14,22},{15,7},{16,24},... | collective-permute-start | bytes 4325384 | tf_op jit(solution)/shard_map/ppermute | solution.py:156
  320.9 34.7 %collective-permute-start.48 = (bf16[1408,512]{1,0:T(8,128)(2,1)}, bf16[1408,512]{1,0:T(8,128)(2,1)}, u32[]{:S(2)}, u32[]{:S(2)}) collective-permute-start(bf16[1408,512]{1,0:T(8,128)(2,1)} %get-tuple-element.382.refs_0_), channel_id=1, source_target_pairs={{0,4},{1,5},{2,6},{3,7},{4,0},{5,1},{6,2},{7,3},{8,12},{9,13},{10,... | collective-permute-start | bytes 4325384 | tf_op jit(solution)/shard_map/ppermute | solution.py:156
  359.1 37.2 %collective-permute-start.52 = (bf16[1408,512]{1,0:T(8,128)(2,1)}, bf16[1408,512]{1,0:T(8,128)(2,1)}, u32[]{:S(2)}, u32[]{:S(2)}) collective-permute-start(bf16[1408,512]{1,0:T(8,128)(2,1)} %get-tuple-element.438.refs_2_), channel_id=1, source_target_pairs={{0,4},{1,5},{2,6},{3,7},{4,0},{5,1},{6,2},{7,3},{8,12},{9,13},{10,... | collective-permute-start | bytes 4325384 | tf_op jit(solution)/shard_map/ppermute | solution.py:156
  359.6 36.6 %collective-permute-start.51 = (bf16[1408,512]{1,0:T(8,128)(2,1)}, bf16[1408,512]{1,0:T(8,128)(2,1)S(1)}, u32[]{:S(2)}, u32[]{:S(2)}) collective-permute-start(bf16[1408,512]{1,0:T(8,128)(2,1)} %get-tuple-element.437), channel_id=1, source_target_pairs={{8,16},{9,1},{10,18},{11,3},{12,20},{13,5},{14,22},{15,7},{16,24},... | collective-permute-start | bytes 4325384 | tf_op jit(solution)/shard_map/ppermute | solution.py:156
  398.3 38.2 %collective-permute-start.55 = (bf16[1408,512]{1,0:T(8,128)(2,1)}, bf16[1408,512]{1,0:T(8,128)(2,1)S(1)}, u32[]{:S(2)}, u32[]{:S(2)}) collective-permute-start(bf16[1408,512]{1,0:T(8,128)(2,1)} %get-tuple-element.436), channel_id=1, source_target_pairs={{8,16},{9,1},{10,18},{11,3},{12,20},{13,5},{14,22},{15,7},{16,24},... | collective-permute-start | bytes 4325384 | tf_op jit(solution)/shard_map/ppermute | solution.py:156
  399.6 36.9 %collective-permute-start.56 = (bf16[1408,512]{1,0:T(8,128)(2,1)}, bf16[1408,512]{1,0:T(8,128)(2,1)}, u32[]{:S(2)}, u32[]{:S(2)}) collective-permute-start(bf16[1408,512]{1,0:T(8,128)(2,1)} %get-tuple-element.406.refs_0_), channel_id=1, source_target_pairs={{0,4},{1,5},{2,6},{3,7},{4,0},{5,1},{6,2},{7,3},{8,12},{9,13},{10,... | collective-permute-start | bytes 4325384 | tf_op jit(solution)/shard_map/ppermute | solution.py:156
  401.2 35.3 %collective-permute-start.57 = (bf16[1408,512]{1,0:T(8,128)(2,1)}, bf16[1408,512]{1,0:T(8,128)(2,1)}, u32[]{:S(2)}, u32[]{:S(2)}) collective-permute-start(bf16[1408,512]{1,0:T(8,128)(2,1)} %get-tuple-element.406.refs_0_), channel_id=1, source_target_pairs={{0,2},{1,3},{2,0},{3,1},{4,6},{5,7},{6,4},{7,5},{8,10},{9,11},{10,... | collective-permute-start | bytes 4325384 | tf_op jit(solution)/shard_map/ppermute | solution.py:156
  438.0 37.7 %collective-permute-start.60 = (bf16[1408,512]{1,0:T(8,128)(2,1)S(1)}, bf16[1408,512]{1,0:T(8,128)(2,1)}, u32[]{:S(2)}, u32[]{:S(2)}) collective-permute-start(bf16[1408,512]{1,0:T(8,128)(2,1)S(1)} %get-tuple-element.434.refs_2_), channel_id=1, source_target_pairs={{0,4},{1,5},{2,6},{3,7},{4,0},{5,1},{6,2},{7,3},{8,12},{9,13},{10,... | collective-permute-start | bytes 4325384 | tf_op jit(solution)/shard_map/ppermute | solution.py:156
  439.5 36.1 %collective-permute-start.59 = (bf16[1408,512]{1,0:T(8,128)(2,1)}, bf16[1408,512]{1,0:T(8,128)(2,1)S(1)}, u32[]{:S(2)}, u32[]{:S(2)}) collective-permute-start(bf16[1408,512]{1,0:T(8,128)(2,1)} %get-tuple-element.433), channel_id=1, source_target_pairs={{8,16},{9,1},{10,18},{11,3},{12,20},{13,5},{14,22},{15,7},{16,24},... | collective-permute-start | bytes 4325384 | tf_op jit(solution)/shard_map/ppermute | solution.py:156
  440.9 34.7 %collective-permute-start.61 = (bf16[1408,512]{1,0:T(8,128)(2,1)}, bf16[1408,512]{1,0:T(8,128)(2,1)S(1)}, u32[]{:S(2)}, u32[]{:S(2)}) collective-permute-start(bf16[1408,512]{1,0:T(8,128)(2,1)} %collective-permute-done.56.refs_0_), channel_id=1, source_target_pairs={{0,2},{1,3},{2,0},{3,1},{4,6},{5,7},{6,4},{7,5},{8,10},{9,11},{10,... | collective-permute-start | bytes 4325384 | tf_op jit(solution)/shard_map/ppermute | solution.py:156
  476.7 36.1 %collective-permute-start.63 = (bf16[1408,512]{1,0:T(8,128)(2,1)S(1)}, bf16[1408,512]{1,0:T(8,128)(2,1)S(1)}, u32[]{:S(2)}, u32[]{:S(2)}) collective-permute-start(bf16[1408,512]{1,0:T(8,128)(2,1)S(1)} %collective-permute-done.59), channel_id=1, source_target_pairs={{9,1},{11,3},{13,5},{15,7},{16,24},{18,26},{20,28},{22,30}} | collective-permute-start | bytes 4325384 | tf_op jit(solution)/shard_map/ppermute | solution.py:156
  478.5 34.3 %collective-permute-start.64 = (bf16[1408,512]{1,0:T(8,128)(2,1)S(1)}, bf16[1408,512]{1,0:T(8,128)(2,1)S(1)}, u32[]{:S(2)}, u32[]{:S(2)}) collective-permute-start(bf16[1408,512]{1,0:T(8,128)(2,1)S(1)} %select_select_fusion.1.refs_0_), channel_id=1, source_target_pairs={{0,4},{1,5},{2,6},{3,7},{4,0},{5,1},{6,2},{7,3},{8,12},{9,13},{10,... | collective-permute-start | bytes 4325384 | tf_op jit(solution)/shard_map/ppermute | solution.py:156
  513.9 40.0 %collective-permute-start.68 = (bf16[1408,512]{1,0:T(8,128)(2,1)S(1)}, bf16[1408,512]{1,0:T(8,128)(2,1)S(1)}, u32[]{:S(2)}, u32[]{:S(2)}) collective-permute-start(bf16[1408,512]{1,0:T(8,128)(2,1)S(1)} %select_select_fusion.refs_2_), channel_id=1, source_target_pairs={{0,4},{1,5},{2,6},{3,7},{4,0},{5,1},{6,2},{7,3},{8,12},{9,13},{10,... | collective-permute-start | bytes 4325384 | tf_op jit(solution)/shard_map/ppermute | solution.py:156
  (90 other events, 1572.1 us)

commit v3 on v2

--- a/solution.py
+++ b/solution.py
@@ -170,16 +170,6 @@
     def z_down(a, step):
         return move(a, lambda z, y, k, x: (z - 1, y, k, x) if 0 < z <= 4 - step else None)
 
-    def u_to(a, steps):
-        def target(z, y, k, x):
-            u = z if x == 0 else 3 - z
-            if u not in steps:
-                return None
-            v = steps[u]
-            return (v if x == 0 else 3 - v), y, k, x
-
-        return move(a, target)
-
     slab_rows = half_slab.shape[0]
     chip_rows = 4 * slab_rows
     rows = chip_rows // 2
@@ -229,7 +219,7 @@
     cuts = [slab_rows * i // SLAB_PARTS // 16 * 16 for i in range(SLAB_PARTS)] + [slab_rows]
 
     def slab_part(i):
-        return {f"slab_x{i}": over_x(env["slab"][cuts[i] : cuts[i + 1]])}
+        return {f"slab_x{i}": over_x(env["slab"][:cuts[1]] if i == 0 else env.pop(f"slab{i}"))}
 
     def slab_part_k(i):
         return {f"slab_kx{i}": over_k(env[f"slab_x{i}"])}
@@ -248,51 +238,72 @@
                     coefs.append(env[f"{prefix}{name}{n}_{c}"] if whole is None else whole)
                     columns.append(k * width + (0 if whole is None else c * both))
                     coef_at.append(((planes[n] * 2 + at_y) * 2 + core) * coef_rows)
-        return {f"own{c}0": transform(groups, group_rows, coefs, coef_at, columns, width)}
+        return {f"own{c}": transform(groups, group_rows, coefs, coef_at, columns, width)}
 
     def panel(c):
         parts = []
         for p, v in ((0, x), (1, 1 - x)):
-            for held, core in ((env[f"own{c}{p}"], k), (env.pop(f"kown{c}{p}"), 1 - k)):
+            name = ("own", "own_x")[p] + str(c)
+            for held, core in ((env[name], k), (env.pop("k" + name), 1 - k)):
                 of_rows = lax.dynamic_slice(held, (k * rows, 0), (rows, width))
                 at = v * virt_x + c * both + core * width
                 scale = lax.dynamic_slice(weights, (0, at), (freqs, width))
                 parts.append((of_rows.astype(F32)[None] * scale[:, None]).astype(BF16))
         return {f"scaled{c}": jnp.concatenate(parts, 2)}
 
-    items = [(c, near, p) for c in range(PARTS) for near in (1, 0) for p in (0, 1)]
-    count = len(items)
-
-    def item(t):
-        c, near, p = items[t]
-        return env[f"own{c}{p}"] if near else env[f"far{c}{p}"]
-
-    def exchange(c, p):
-        return {f"far{c}{p}": u_to(env[f"own{c}{p}"], {0: 1, 1: 0})}
-
-    def along(t):
-        if t == 0:
-            return {"got0": u_to(item(0), {1: 2})}
-        if t == count:
-            return {f"got{t}": u_to(env[f"got{t - 1}"], {2: 3})}
-        return {f"got{t}": u_to(jnp.where(u == 1, item(t), env[f"got{t - 1}"]), {1: 2, 2: 3})}
-
-    def take(t):
-        held = jnp.where(u <= 1, item(t), jnp.where(u == 2, env[f"got{t}"], env[f"got{t + 1}"]))
-        return {f"a{t}": held, f"b{t}": over_y(held), f"ka{t}": over_k(held)}
-
-    def taken(t):
-        return {f"kb{t}": over_k(env[f"b{t}"])}
-
-    def block(t, crossed, pieces_of, part, first):
-        c, near, _ = items[t]
+    home = u <= 1
+    inner = (z == 1) | (z == 2)
+
+    def planes_swap(a, pairs):
+        return move(a, lambda z, y, k, x: (pairs[z], y, k, x) if z in pairs else None)
+
+    def to_visitor(a):
+        return move(a, lambda z, y, k, x: (z, y, k, 1 - x) if x == z // 2 else None)
+
+    def here(s):
+        return env[f"{('own', 'far')[s % 2]}{s // 2}"]
+
+    def inward(s):
+        return {f"mid{s}": planes_swap(here(s), {1: 2, 2: 1})}
+
+    def outward(s):
+        return {f"out{s}": planes_swap(env[f"mid{s}"], {1: 0, 2: 3})}
+
+    def exchange(c):
+        return {f"far{c}": planes_swap(env[f"own{c}"], {0: 1, 1: 0, 2: 3, 3: 2})}
+
+    def own_x(c):
+        return {f"own_x{c}": over_x(env[f"own{c}"])}
+
+    def choose(s):
+        visiting = jnp.where(inner, env.pop(f"mid{s}"), env.pop(f"out{s}"))
+        env[f"o{s}"] = jnp.where(home, here(s), visiting)
+        if s % 2:
+            return {f"c{s}": over_x(jnp.where(home, visiting, here(s)))}
+        return {f"x{s}": to_visitor(visiting)}
+
+    def join(s):
+        env[f"c{s}"] = jnp.where(home, env[f"own_x{s // 2}"], env.pop(f"x{s}"))
+
+    def cross_y(name):
+        return {f"y{name}": over_y(env[name])}
+
+    def cross_core(*names):
+        return {f"k{name}": over_k(env[name]) for name in names}
+
+    def block(s, crossed, new):
+        env.update(new)
+        near = 1 - s % 2
         plane = jnp.where(u == 0, 1 - near, near)
         plane = jnp.where(x == 0, plane, 1 - plane)
         place = plane * 2 + (1 - y if crossed else y)
-        env["out"] = add_block(env.get("out"), shape, place, env[f"scaled{c}"], pieces_of, part, first)
+        names = [f"{q}{p}{s}" for p in (("yo", "yc") if crossed else ("o", "c")) for q in ("", "k")]
+        pieces = [env.pop(n) if crossed or n[0] == "k" else env[n] for n in names]
+        env["out"] = add_block(env.get("out"), shape, place, env[f"scaled{s // 2}"], pieces, 0, s < 2)
 
     env["coef"], env["slab"] = coef, half_slab
-    step(**line(1), **cross(0), **slab_part(0), slab_k=over_k(env["slab"]))
+    parts = {f"slab{i}": env["slab"][cuts[i] : cuts[i + 1]] for i in range(1, SLAB_PARTS)}
+    step(**line(1), **cross(0), **slab_part(0), **parts, slab_k=over_k(env["slab"]))
     step(**line(2), **cross(1), **slab_part(1), **slab_part_k(0), **cross_k(0))
     step(**line(3), **cross(2), **slab_part(2), **slab_part_k(1), **cross_k(1))
     env["slot3"] = slot(3)
@@ -302,38 +313,33 @@
     env["kcross3_0"] = over_k(env["cross3_0"])
     step(**transformed(0))
 
-    for t in range(count + 2):
-        r = along(t) if t <= count else {}
-        if t == 0:
-            r |= dict(cross3_1=over_y(env.pop("later")))
-            r |= dict(own01=over_x(env["own00"]), kown00=over_k(env["own00"])) | exchange(0, 0)
-        if t == 1:
-            env["kcross3_1"] = over_k(env["cross3_1"])
-            r |= dict(kown01=over_k(env["own01"])) | exchange(0, 1)
-            r |= transformed(1)
-        if t == 2:
-            r |= panel(0) | exchange(1, 0)
-            r |= dict(own11=over_x(env["own10"]), kown10=over_k(env["own10"]))
-        if t == 3:
-            r |= dict(kown11=over_k(env["own11"])) | exchange(1, 1)
-        if t == 5:
-            r |= panel(1)
-        if t >= 2:
-            r |= take(t - 2)
-        if t >= 3:
-            r |= taken(t - 3)
-        if t >= 3 and t % 2 == 1:
-            i = t - 3
-            pieces = [env.pop(f"a{i}"), env.pop(f"ka{i}"), r.pop(f"a{i + 1}"), r.pop(f"ka{i + 1}")]
-            block(i, False, pieces, 0, i < count // PARTS)
-        if t >= 4 and t % 2 == 0:
-            i = t - 4
-            pieces = [env.pop(f"b{i}"), env.pop(f"kb{i}"), env.pop(f"b{i + 1}"), r.pop(f"kb{i + 1}")]
-            block(i, True, pieces, 0, i < count // PARTS)
-        if t == count + 1:
-            block(count - 2, True, [env.pop(f"b{count - 2}"), r.pop(f"kb{count - 2}")], 0, False)
-        step(**r)
-    block(count - 2, True, [env[f"b{count - 1}"], taken(count - 1)[f"kb{count - 1}"]], 1, False)
+    first = inward(0) | exchange(0) | own_x(0) | cross_core("own0")
+    env["cross3_1"] = over_y(env.pop("later"))
+    env["kcross3_1"] = over_k(env["cross3_1"])
+    step(**first, **transformed(1))
+    step(**inward(1), **outward(0), **own_x(1), **cross_core("own1", "own_x0"))
+    r = choose(0) | cross_y("o0") | cross_core("o0", "own_x1")
+    step(**r, **inward(2), **exchange(1), **panel(0))
+    join(0)
+    r = cross_y("c0") | inward(3) | outward(1) | cross_core("yo0")
+    block(0, False, cross_core("c0"))
+    step(**r)
+    r = choose(1) | cross_y("o1") | outward(2) | cross_core("o1")
+    block(0, True, cross_core("yc0"))
+    step(**r)
+    r = choose(2) | cross_y("c1") | outward(3) | cross_core("o2", "yo1") | panel(1)
+    block(1, False, cross_core("c1"))
+    step(**r)
+    join(2)
+    r = cross_y("o2") | cross_y("c2") | choose(3) | cross_core("o3")
+    block(1, True, cross_core("yc1"))
+    block(2, False, cross_core("c2"))
+    step(**r)
+    r = cross_y("o3") | cross_y("c3")
+    block(3, False, cross_core("c3"))
+    block(2, True, cross_core("yo2", "yc2"))
+    step(**r)
+    block(3, True, cross_core("yo3", "yc3"))
     return env["out"]
 
 

time: 582 us -> 551 us (0.947)
  waiting for transfers between devices: 262 us -> 248 us
  Pallas kernels: 194 us -> 183 us
  other arithmetic: 39.8 us -> 31.6 us
  starting transfers between devices: 57.9 us -> 65.7 us
    ppermute x70 -> x71, waiting for transfers between devices: 262 us -> 248 us  [move(): return lax.ppermute(array, AXES, pairs)]
    pallas_call x9 -> x8, Pallas kernels: 168 us -> 158 us  [add_block(): pl.pallas_call(functools.partial(block_kernel, n_pieces=len(pieces), firs...]
    select_n x9 -> x6, other arithmetic: 17.7 us -> 8.48 us  [the longest x2 4.84 us: choose(): return {f'c{s}': over_x(jnp.where(home, visiting, here(s)))}]
    ppermute x70 -> x71, starting transfers between devices: 57.9 us -> 65.7 us  [move(): return lax.ppermute(array, AXES, pairs)]
  transfers between devices with their start and end apart: 70 -> 71, of which waited for: 28 -> 29; matrix products, arithmetic and copies ran while one was open for 6% -> 6% of each run, Pallas kernels for 29% -> 28%
where the time goes in v3:
time: 551 us; the launch traced here: 546 us
  waiting for transfers between devices  248 us (45%)
  Pallas kernels  183 us (33%)
  starting transfers between devices  65.7 us (12%)
  other arithmetic  31.6 us (6%)
  local copies, waits for them, and re-layouts  15.2 us (3%)
    ppermute x71, waiting for transfers between devices, move(): return lax.ppermute(array, AXES, pairs)  248 us
    pallas_call x8, Pallas kernels, add_block(): pl.pallas_call(functools.partial(block_kernel, n_pieces=len(pieces), firs...  158 us
    ppermute x71, starting transfers between devices, move(): return lax.ppermute(array, AXES, pairs)  65.7 us
    pallas_call x2, Pallas kernels, transform(): pl.pallas_call(functools.partial(transform_kernel, counts=[len(g) for g i...  25.5 us
  transfers between devices with their start and end apart: 71, of which 29 were waited for; matrix products, arithmetic and copies ran while one was open for 6% of the time, Pallas kernels for 28%

profile of v3, /device:TPU:2, one launch (start us, length us, event | category | flops | bytes accessed | tf_op | source)
XLA Modules:
  0.0 545.5 jit_solution(8718933046265449492)
XLA Ops:
  10.8 17.3 %collective-permute-done.4.refs_2_ = bf16[112,4608]{1,0:T(8,128)(2,1)} collective-permute-done((bf16[112,4608]{1,0:T(8,128)(2,1)S(1)}, bf16[112,4608]{1,0:T(8,128)(2,1)}, u32[]{:S(2)}, u32[]{:S(2)}) %collective-permute-start.4) | collective-permute-done | bytes 1032224 | tf_op jit(solution)/shard_map/ppermute | solution.py:156
  32.4 5.3 collective-permute-done.1
  46.2 16.5 %collective-permute-done.10.refs_3_ = bf16[112,4608]{1,0:T(8,128)(2,1)} collective-permute-done((bf16[112,4608]{1,0:T(8,128)(2,1)}, bf16[112,4608]{1,0:T(8,128)(2,1)}, u32[]{:S(2)}, u32[]{:S(2)}) %collective-permute-start.10) | collective-permute-done | bytes 1032224 | tf_op jit(solution)/shard_map/ppermute | solution.py:156
  63.3 10.6 %collective-permute-done.7 = bf16[288,2048]{1,0:T(8,128)(2,1)S(1)} collective-permute-done((bf16[288,2048]{1,0:T(8,128)(2,1)}, bf16[288,2048]{1,0:T(8,128)(2,1)S(1)}, u32[]{:S(2)}, u32[]{:S(2)}) %collective-permute-start.7) | collective-permute-done | bytes 1179680 | tf_op jit(solution)/shard_map/ppermute | solution.py:156
  82.3 25.7 %collective-permute-done.14 = bf16[288,2048]{1,0:T(8,128)(2,1)} collective-permute-done((bf16[288,2048]{1,0:T(8,128)(2,1)}, bf16[288,2048]{1,0:T(8,128)(2,1)}, u32[]{:S(2)}, u32[]{:S(2)}) %collective-permute-start.14) | collective-permute-done | bytes 1179680 | tf_op jit(solution)/shard_map/ppermute | solution.py:156
  113.4 15.2 %collective-permute-done.20.refs_22_ = bf16[288,1024]{1,0:T(8,128)(2,1)S(1)} collective-permute-done((bf16[288,1024]{1,0:T(8,128)(2,1)S(1)}, bf16[288,1024]{1,0:T(8,128)(2,1)S(1)}, u32[]{:S(2)}, u32[]{:S(2)}) %collective-permute-start.20) | collective-permute-done | bytes 589856 | tf_op jit(solution)/shard_map/ppermute | solution.py:156
  131.8 12.8 %shard_map.55 = bf16[1408,512]{1,0:T(8,128)(2,1)} custom-call(s32[36]{0:T(128)} %stack.69.at, bf16[352,4608]{1,0:T(8,128)(2,1)} %refs_0_.1, bf16[352,4608]{1,0:T(8,128)(2,1)} %collective-permute-done.5.refs_1_, bf16[112,4608]{1,0:T(8,128)(2,1)} %collective-permute-done.4.refs_2_, bf16[112,4608]{1,0:T(8,128)(2,1)} %collective-permute-done.10.refs_3_, ...), custom_call_target="tpu_custom_call" | custom-call | flops 6643777536 | bytes 17694720 | tf_op jit(solution)/shard_map/pallas_call | solution.py:74
  152.8 7.2 %collective-permute-done.25.refs_22_ = bf16[288,1024]{1,0:T(8,128)(2,1)S(1)} collective-permute-done((bf16[288,1024]{1,0:T(8,128)(2,1)S(1)}, bf16[288,1024]{1,0:T(8,128)(2,1)S(1)}, u32[]{:S(2)}, u32[]{:S(2)}) %collective-permute-start.25) | collective-permute-done | bytes 589856 | tf_op jit(solution)/shard_map/ppermute | solution.py:156
  162.8 12.7 %shard_map.56 = bf16[1408,512]{1,0:T(8,128)(2,1)} custom-call(s32[36]{0:T(128)} %stack.71.at, bf16[352,4608]{1,0:T(8,128)(2,1)} %refs_0_.1, bf16[352,4608]{1,0:T(8,128)(2,1)} %collective-permute-done.5.refs_1_, bf16[112,4608]{1,0:T(8,128)(2,1)} %collective-permute-done.4.refs_2_, bf16[112,4608]{1,0:T(8,128)(2,1)} %collective-permute-done.10.refs_3_, ...), custom_call_target="tpu_custom_call" | custom-call | flops 6643777536 | bytes 17694720 | tf_op jit(solution)/shard_map/pallas_call | solution.py:74
  175.6 8.3 %collective-permute-done.28 = bf16[1408,512]{1,0:T(8,128)(2,1)} collective-permute-done((bf16[1408,512]{1,0:T(8,128)(2,1)}, bf16[1408,512]{1,0:T(8,128)(2,1)}, u32[]{:S(2)}, u32[]{:S(2)}) %collective-permute-start.28) | collective-permute-done | bytes 1441824 | tf_op jit(solution)/shard_map/ppermute | solution.py:156
  190.5 30.7 %collective-permute-done.32 = bf16[1408,512]{1,0:T(8,128)(2,1)} collective-permute-done((bf16[1408,512]{1,0:T(8,128)(2,1)}, bf16[1408,512]{1,0:T(8,128)(2,1)}, u32[]{:S(2)}, u32[]{:S(2)}) %collective-permute-start.32) | collective-permute-done | bytes 1441824 | tf_op jit(solution)/shard_map/ppermute | solution.py:156
  235.2 20.4 %collective-permute-done.36 = bf16[1408,512]{1,0:T(8,128)(2,1)S(1)} collective-permute-done((bf16[1408,512]{1,0:T(8,128)(2,1)S(1)}, bf16[1408,512]{1,0:T(8,128)(2,1)S(1)}, u32[]{:S(2)}, u32[]{:S(2)}) %collective-permute-start.36) | collective-permute-done | bytes 1441824 | tf_op jit(solution)/shard_map/ppermute | solution.py:156
  269.1 19.2 %shard_map.57.refs_4_ = f32[3,704,5632]{2,1,0:T(8,128)} custom-call(s32[1]{0:T(128)} %bitcast.25.place, bf16[3,704,2048]{2,1,0:T(8,128)(2,1)} %pad_maximum_fusion.scaled, bf16[1408,512]{1,0:T(8,128)(2,1)} %copy-done.7, bf16[1408,512]{1,0:T(8,128)(2,1)} %copy-done.25, bf16[1408,512]{1,0:T(8,128)(2,1)} %copy-done.6, ...), custom_call_target="tpu_custom_call" | custom-call | flops 12180258816 | bytes 26312704 | tf_op jit(solution)/shard_map/pallas_call | solution.py:123
  288.3 10.7 %collective-permute-done.43.refs_2_ = bf16[1408,512]{1,0:T(8,128)(2,1)} collective-permute-done((bf16[1408,512]{1,0:T(8,128)(2,1)S(1)}, bf16[1408,512]{1,0:T(8,128)(2,1)}, u32[]{:S(2)}, u32[]{:S(2)}) %collective-permute-start.43) | collective-permute-done | bytes 1441824 | tf_op jit(solution)/shard_map/ppermute | solution.py:156
  311.8 19.2 %shard_map.58.refs_4_ = f32[3,704,5632]{2,1,0:T(8,128)} custom-call(s32[1]{0:T(128)} %bitcast.1.place, bf16[3,704,2048]{2,1,0:T(8,128)(2,1)} %pad_maximum_fusion.scaled, bf16[1408,512]{1,0:T(8,128)(2,1)} %collective-permute-done.37.refs_0_, bf16[1408,512]{1,0:T(8,128)(2,1)} %collective-permute-done.46.refs_1_, ...), custom_call_target="tpu_custom_call", output_to_operand_aliasing={{}: (6, {})} | custom-call | flops 12180258816 | bytes 26312704 | tf_op jit(solution)/shard_map/pallas_call | solution.py:123
  331.0 10.5 %collective-permute-done.48.refs_2_ = bf16[1408,512]{1,0:T(8,128)(2,1)} collective-permute-done((bf16[1408,512]{1,0:T(8,128)(2,1)}, bf16[1408,512]{1,0:T(8,128)(2,1)}, u32[]{:S(2)}, u32[]{:S(2)}) %collective-permute-start.48) | collective-permute-done | bytes 1441824 | tf_op jit(solution)/shard_map/ppermute | solution.py:156
  360.4 19.1 %shard_map.59.refs_4_ = f32[3,704,5632]{2,1,0:T(8,128)} custom-call(s32[1]{0:T(128)} %bitcast.26.place, bf16[3,704,2048]{2,1,0:T(8,128)(2,1)} %pad_maximum_fusion.scaled, bf16[1408,512]{1,0:T(8,128)(2,1)} %copy-done.9, bf16[1408,512]{1,0:T(8,128)(2,1)} %collective-permute-done.51.refs_1_, ...), custom_call_target="tpu_custom_call", output_to_operand_aliasing={{}: (6, {})} | custom-call | flops 12180258816 | bytes 26312704 | tf_op jit(solution)/shard_map/pallas_call | solution.py:123
  396.3 19.2 %shard_map.60.refs_4_ = f32[3,704,5632]{2,1,0:T(8,128)} custom-call(s32[1]{0:T(128)} %bitcast.place, bf16[3,704,2048]{2,1,0:T(8,128)(2,1)} %pad_maximum_fusion.scaled, bf16[1408,512]{1,0:T(8,128)(2,1)} %collective-permute-done.49.refs_0_, bf16[1408,512]{1,0:T(8,128)(2,1)} %collective-permute-done.57.refs_1_, ...), custom_call_target="tpu_custom_call", output_to_operand_aliasing={{}: (6, {})} | custom-call | flops 12180258816 | bytes 26312704 | tf_op jit(solution)/shard_map/pallas_call | solution.py:123
  415.5 20.3 %shard_map.61.refs_4_ = f32[3,704,5632]{2,1,0:T(8,128)} custom-call(s32[1]{0:T(128)} %bitcast.25.place, bf16[3,704,2048]{2,1,0:T(8,128)(2,1)} %pad_maximum_fusion.1.scaled, bf16[1408,512]{1,0:T(8,128)(2,1)} %copy-done.8, bf16[1408,512]{1,0:T(8,128)(2,1)} %copy-done.24, bf16[1408,512]{1,0:T(8,128)(2,1)} %copy-done.5, ...), custom_call_target="tpu_custom_call", output_to_operand_aliasing={{}: (6, {})} | custom-call | flops 12180258816 | bytes 38207488 | tf_op jit(solution)/shard_map/pallas_call | solution.py:123
  435.8 17.4 %collective-permute-done.60.refs_0_ = bf16[1408,512]{1,0:T(8,128)(2,1)} collective-permute-done((bf16[1408,512]{1,0:T(8,128)(2,1)S(1)}, bf16[1408,512]{1,0:T(8,128)(2,1)}, u32[]{:S(2)}, u32[]{:S(2)}) %collective-permute-start.60) | collective-permute-done | bytes 1441824 | tf_op jit(solution)/shard_map/ppermute | solution.py:156
  457.9 20.3 %shard_map.62.refs_4_ = f32[3,704,5632]{2,1,0:T(8,128)} custom-call(s32[1]{0:T(128)} %bitcast.26.place, bf16[3,704,2048]{2,1,0:T(8,128)(2,1)} %pad_maximum_fusion.1.scaled, bf16[1408,512]{1,0:T(8,128)(2,1)} %copy-done.10, bf16[1408,512]{1,0:T(8,128)(2,1)} %collective-permute-done.63.refs_1_, ...), custom_call_target="tpu_custom_call", output_to_operand_aliasing={{}: (6, {})} | custom-call | flops 12180258816 | bytes 38207488 | tf_op jit(solution)/shard_map/pallas_call | solution.py:123
  479.4 20.3 %shard_map.63.refs_4_ = f32[3,704,5632]{2,1,0:T(8,128)} custom-call(s32[1]{0:T(128)} %bitcast.1.place, bf16[3,704,2048]{2,1,0:T(8,128)(2,1)} %pad_maximum_fusion.1.scaled, bf16[1408,512]{1,0:T(8,128)(2,1)} %collective-permute-done.60.refs_0_, bf16[1408,512]{1,0:T(8,128)(2,1)} %copy-done.30, ...), custom_call_target="tpu_custom_call", output_to_operand_aliasing={{}: (6, {})} | custom-call | flops 12180258816 | bytes 38207488 | tf_op jit(solution)/shard_map/pallas_call | solution.py:123
  499.7 19.1 %collective-permute-done.67.refs_0_ = bf16[1408,512]{1,0:T(8,128)(2,1)S(1)} collective-permute-done((bf16[1408,512]{1,0:T(8,128)(2,1)S(1)}, bf16[1408,512]{1,0:T(8,128)(2,1)S(1)}, u32[]{:S(2)}, u32[]{:S(2)}) %collective-permute-start.67) | collective-permute-done | bytes 1441824 | tf_op jit(solution)/shard_map/ppermute | solution.py:156
  525.2 20.3 %shard_map.64 = f32[3,704,5632]{2,1,0:T(8,128)} custom-call(s32[1]{0:T(128)} %bitcast.place, bf16[3,704,2048]{2,1,0:T(8,128)(2,1)} %pad_maximum_fusion.1.scaled, bf16[1408,512]{1,0:T(8,128)(2,1)} %copy-done.29, bf16[1408,512]{1,0:T(8,128)(2,1)} %copy-done.31, bf16[1408,512]{1,0:T(8,128)(2,1)} %copy-done.28, ...), custom_call_target="tpu_custom_call", output_to_operand_aliasing={{}: (6, {})} | custom-call | flops 12180258816 | bytes 38207488 | tf_op jit(solution)/shard_map/pallas_call | solution.py:123
  (242 shorter events, 145.6 us)
Async XLA Ops:
  0.0 38.7 %collective-permute-start.5 = (bf16[352,4608]{1,0:T(8,128)(2,1)}, bf16[352,4608]{1,0:T(8,128)(2,1)}, u32[]{:S(2)}, u32[]{:S(2)}) collective-permute-start(bf16[352,4608]{1,0:T(8,128)(2,1)} %refs_0_.1), channel_id=1, source_target_pairs={{0,2},{1,3},{2,0},{3,1},{4,6},{5,7},{6,4},{7,5},{8,10},{9,11},{10,... | collective-permute-start | bytes 9732104 | tf_op jit(solution)/shard_map/ppermute | solution.py:156
  147.0 36.9 %collective-permute-start.28 = (bf16[1408,512]{1,0:T(8,128)(2,1)}, bf16[1408,512]{1,0:T(8,128)(2,1)}, u32[]{:S(2)}, u32[]{:S(2)}) collective-permute-start(bf16[1408,512]{1,0:T(8,128)(2,1)} %shard_map.55), channel_id=1, source_target_pairs={{0,8},{1,9},{2,10},{3,11},{4,12},{5,13},{6,14},{7,15},{8,0},{9,1},... | collective-permute-start | bytes 4325384 | tf_op jit(solution)/shard_map/ppermute | solution.py:156
  187.1 34.0 %collective-permute-start.32 = (bf16[1408,512]{1,0:T(8,128)(2,1)}, bf16[1408,512]{1,0:T(8,128)(2,1)}, u32[]{:S(2)}, u32[]{:S(2)}) collective-permute-start(bf16[1408,512]{1,0:T(8,128)(2,1)} %collective-permute-done.27), channel_id=1, source_target_pairs={{8,0},{9,1},{10,2},{11,3},{12,4},{13,5},{14,6},{15,7},{16,24},{17,... | collective-permute-start | bytes 4325384 | tf_op jit(solution)/shard_map/ppermute | solution.py:156
  224.3 37.9 %collective-permute-start.37 = (bf16[1408,512]{1,0:T(8,128)(2,1)S(1)}, bf16[1408,512]{1,0:T(8,128)(2,1)}, u32[]{:S(2)}, u32[]{:S(2)}) collective-permute-start(bf16[1408,512]{1,0:T(8,128)(2,1)S(1)} %get-tuple-element.304.refs_0_), channel_id=1, source_target_pairs={{0,4},{1,5},{2,6},{3,7},{4,0},{5,1},{6,2},{7,3},{8,12},{9,13},{10,... | collective-permute-start | bytes 4325384 | tf_op jit(solution)/shard_map/ppermute | solution.py:156
  225.9 36.3 %collective-permute-start.38 = (bf16[1408,512]{1,0:T(8,128)(2,1)S(1)}, bf16[1408,512]{1,0:T(8,128)(2,1)S(1)}, u32[]{:S(2)}, u32[]{:S(2)}) collective-permute-start(bf16[1408,512]{1,0:T(8,128)(2,1)S(1)} %get-tuple-element.304.refs_0_), channel_id=1, source_target_pairs={{0,2},{1,3},{2,0},{3,1},{4,6},{5,7},{6,4},{7,5},{8,10},{9,11},{10,... | collective-permute-start | bytes 4325384 | tf_op jit(solution)/shard_map/ppermute | solution.py:156
  225.9 36.4 %collective-permute-start.40 = (bf16[1408,512]{1,0:T(8,128)(2,1)S(1)}, bf16[1408,512]{1,0:T(8,128)(2,1)}, u32[]{:S(2)}, u32[]{:S(2)}) collective-permute-start(bf16[1408,512]{1,0:T(8,128)(2,1)S(1)} %copy-done.4), channel_id=1, source_target_pairs={{8,16},{9,17},{10,18},{11,19},{12,20},{13,21},{14,22},{15,23},{16,... | collective-permute-start | bytes 4325384 | tf_op jit(solution)/shard_map/ppermute | solution.py:156
  227.7 37.0 %collective-permute-start.41 = (bf16[1408,512]{1,0:T(8,128)(2,1)S(1)}, bf16[1408,512]{1,0:T(8,128)(2,1)}, u32[]{:S(2)}, u32[]{:S(2)}) collective-permute-start(bf16[1408,512]{1,0:T(8,128)(2,1)S(1)} %copy-done.4), channel_id=1, source_target_pairs={{0,8},{1,9},{2,10},{3,11},{4,12},{5,13},{6,14},{7,15},{8,0},{9,1},... | collective-permute-start | bytes 4325384 | tf_op jit(solution)/shard_map/ppermute | solution.py:156
  264.9 34.1 %collective-permute-start.43 = (bf16[1408,512]{1,0:T(8,128)(2,1)S(1)}, bf16[1408,512]{1,0:T(8,128)(2,1)}, u32[]{:S(2)}, u32[]{:S(2)}) collective-permute-start(bf16[1408,512]{1,0:T(8,128)(2,1)S(1)} %broadcast_select_fusion.10.refs_2_), channel_id=1, source_target_pairs={{0,4},{1,5},{2,6},{3,7},{4,0},{5,1},{6,2},{7,3},{8,12},{9,13},{10,... | collective-permute-start | bytes 4325384 | tf_op jit(solution)/shard_map/ppermute | solution.py:156
  267.7 36.3 %collective-permute-start.45 = (bf16[1408,512]{1,0:T(8,128)(2,1)}, bf16[1408,512]{1,0:T(8,128)(2,1)}, u32[]{:S(2)}, u32[]{:S(2)}) collective-permute-start(bf16[1408,512]{1,0:T(8,128)(2,1)} %collective-permute-done.31), channel_id=1, source_target_pairs={{8,0},{9,1},{10,2},{11,3},{12,4},{13,5},{14,6},{15,7},{16,24},{17,... | collective-permute-start | bytes 4325384 | tf_op jit(solution)/shard_map/ppermute | solution.py:156
  269.0 35.0 %collective-permute-start.46 = (bf16[1408,512]{1,0:T(8,128)(2,1)}, bf16[1408,512]{1,0:T(8,128)(2,1)}, u32[]{:S(2)}, u32[]{:S(2)}) collective-permute-start(bf16[1408,512]{1,0:T(8,128)(2,1)} %collective-permute-done.37.refs_0_), channel_id=1, source_target_pairs={{0,2},{1,3},{2,0},{3,1},{4,6},{5,7},{6,4},{7,5},{8,10},{9,11},{10,... | collective-permute-start | bytes 4325384 | tf_op jit(solution)/shard_map/ppermute | solution.py:156
  307.2 34.3 %collective-permute-start.48 = (bf16[1408,512]{1,0:T(8,128)(2,1)}, bf16[1408,512]{1,0:T(8,128)(2,1)}, u32[]{:S(2)}, u32[]{:S(2)}) collective-permute-start(bf16[1408,512]{1,0:T(8,128)(2,1)} %get-tuple-element.371), channel_id=1, source_target_pairs={{0,1},{1,0},{2,3},{3,2},{4,5},{5,4},{6,7},{7,6},{8,9},{9,8},{10,11... | collective-permute-start | bytes 4325384 | tf_op jit(solution)/shard_map/ppermute | solution.py:156
  308.9 33.8 %collective-permute-start.49 = (bf16[1408,512]{1,0:T(8,128)(2,1)S(1)}, bf16[1408,512]{1,0:T(8,128)(2,1)}, u32[]{:S(2)}, u32[]{:S(2)}) collective-permute-start(bf16[1408,512]{1,0:T(8,128)(2,1)S(1)} %get-tuple-element.331.refs_0_), channel_id=1, source_target_pairs={{0,4},{1,5},{2,6},{3,7},{4,0},{5,1},{6,2},{7,3},{8,12},{9,13},{10,... | collective-permute-start | bytes 4325384 | tf_op jit(solution)/shard_map/ppermute | solution.py:156
  310.4 35.6 %collective-permute-start.50 = (bf16[1408,512]{1,0:T(8,128)(2,1)}, bf16[1408,512]{1,0:T(8,128)(2,1)}, u32[]{:S(2)}, u32[]{:S(2)}) collective-permute-start(bf16[1408,512]{1,0:T(8,128)(2,1)} %collective-permute-done.40), channel_id=1, source_target_pairs={{8,0},{9,1},{10,2},{11,3},{12,4},{13,5},{14,6},{15,7},{16,24},{17,... | collective-permute-start | bytes 4325384 | tf_op jit(solution)/shard_map/ppermute | solution.py:156
  311.7 34.3 %collective-permute-start.51 = (bf16[1408,512]{1,0:T(8,128)(2,1)S(1)}, bf16[1408,512]{1,0:T(8,128)(2,1)}, u32[]{:S(2)}, u32[]{:S(2)}) collective-permute-start(bf16[1408,512]{1,0:T(8,128)(2,1)S(1)} %get-tuple-element.331.refs_0_), channel_id=1, source_target_pairs={{0,2},{1,3},{2,0},{3,1},{4,6},{5,7},{6,4},{7,5},{8,10},{9,11},{10,... | collective-permute-start | bytes 4325384 | tf_op jit(solution)/shard_map/ppermute | solution.py:156
  346.1 38.1 %collective-permute-start.54 = (bf16[1408,512]{1,0:T(8,128)(2,1)}, bf16[1408,512]{1,0:T(8,128)(2,1)}, u32[]{:S(2)}, u32[]{:S(2)}) collective-permute-start(bf16[1408,512]{1,0:T(8,128)(2,1)} %collective-permute-done.48.refs_2_), channel_id=1, source_target_pairs={{0,4},{1,5},{2,6},{3,7},{4,0},{5,1},{6,2},{7,3},{8,12},{9,13},{10,... | collective-permute-start | bytes 4325384 | tf_op jit(solution)/shard_map/ppermute | solution.py:156
  348.5 35.6 %collective-permute-start.53 = (bf16[1408,512]{1,0:T(8,128)(2,1)S(1)}, bf16[1408,512]{1,0:T(8,128)(2,1)S(1)}, u32[]{:S(2)}, u32[]{:S(2)}) collective-permute-start(bf16[1408,512]{1,0:T(8,128)(2,1)S(1)} %get-tuple-element.366), channel_id=1, source_target_pairs={{0,1},{2,3},{4,5},{6,7},{8,9},{10,11},{12,13},{14,15},{17,16},{19,... | collective-permute-start | bytes 4325384 | tf_op jit(solution)/shard_map/ppermute | solution.py:156
  349.8 35.8 %collective-permute-start.55 = (bf16[1408,512]{1,0:T(8,128)(2,1)}, bf16[1408,512]{1,0:T(8,128)(2,1)S(1)}, u32[]{:S(2)}, u32[]{:S(2)}) collective-permute-start(bf16[1408,512]{1,0:T(8,128)(2,1)} %collective-permute-done.44), channel_id=1, source_target_pairs={{8,0},{9,1},{10,2},{11,3},{12,4},{13,5},{14,6},{15,7},{16,24},{17,... | collective-permute-start | bytes 4325384 | tf_op jit(solution)/shard_map/ppermute | solution.py:156
  351.1 34.5 %collective-permute-start.56 = (bf16[1408,512]{1,0:T(8,128)(2,1)S(1)}, bf16[1408,512]{1,0:T(8,128)(2,1)S(1)}, u32[]{:S(2)}, u32[]{:S(2)}) collective-permute-start(bf16[1408,512]{1,0:T(8,128)(2,1)S(1)} %get-tuple-element.345.refs_0_), channel_id=1, source_target_pairs={{0,2},{1,3},{2,0},{3,1},{4,6},{5,7},{6,4},{7,5},{8,10},{9,11},{10,... | collective-permute-start | bytes 4325384 | tf_op jit(solution)/shard_map/ppermute | solution.py:156
  388.7 64.6 %collective-permute-start.61 = (bf16[1408,512]{1,0:T(8,128)(2,1)S(1)}, bf16[1408,512]{1,0:T(8,128)(2,1)}, u32[]{:S(2)}, u32[]{:S(2)}) collective-permute-start(bf16[1408,512]{1,0:T(8,128)(2,1)S(1)} %broadcast_select_fusion.6.refs_2_), channel_id=1, source_target_pairs={{0,4},{1,5},{2,6},{3,7},{4,0},{5,1},{6,2},{7,3},{8,12},{9,13},{10,... | collective-permute-start | bytes 4325384 | tf_op jit(solution)/shard_map/ppermute | solution.py:156
  390.2 63.1 %collective-permute-start.60 = (bf16[1408,512]{1,0:T(8,128)(2,1)S(1)}, bf16[1408,512]{1,0:T(8,128)(2,1)}, u32[]{:S(2)}, u32[]{:S(2)}) collective-permute-start(bf16[1408,512]{1,0:T(8,128)(2,1)S(1)} %get-tuple-element.345.refs_0_), channel_id=1, source_target_pairs={{0,4},{1,5},{2,6},{3,7},{4,0},{5,1},{6,2},{7,3},{8,12},{9,13},{10,... | collective-permute-start | bytes 4325384 | tf_op jit(solution)/shard_map/ppermute | solution.py:156
  392.3 60.9 %collective-permute-start.62 = (bf16[1408,512]{1,0:T(8,128)(2,1)S(1)}, bf16[1408,512]{1,0:T(8,128)(2,1)S(1)}, u32[]{:S(2)}, u32[]{:S(2)}) collective-permute-start(bf16[1408,512]{1,0:T(8,128)(2,1)S(1)} %get-tuple-element.369), channel_id=1, source_target_pairs={{0,1},{1,0},{2,3},{3,2},{4,5},{5,4},{6,7},{7,6},{8,9},{9,8},{10,11... | collective-permute-start | bytes 4325384 | tf_op jit(solution)/shard_map/ppermute | solution.py:156
  396.3 56.9 %collective-permute-start.63 = (bf16[1408,512]{1,0:T(8,128)(2,1)S(1)}, bf16[1408,512]{1,0:T(8,128)(2,1)}, u32[]{:S(2)}, u32[]{:S(2)}) collective-permute-start(bf16[1408,512]{1,0:T(8,128)(2,1)S(1)} %get-tuple-element.357.refs_0_), channel_id=1, source_target_pairs={{0,2},{1,3},{2,0},{3,1},{4,6},{5,7},{6,4},{7,5},{8,10},{9,11},{10,... | collective-permute-start | bytes 4325384 | tf_op jit(solution)/shard_map/ppermute | solution.py:156
  453.9 64.8 %collective-permute-start.68 = (bf16[1408,512]{1,0:T(8,128)(2,1)S(1)}, bf16[1408,512]{1,0:T(8,128)(2,1)S(1)}, u32[]{:S(2)}, u32[]{:S(2)}) collective-permute-start(bf16[1408,512]{1,0:T(8,128)(2,1)S(1)} %collective-permute-done.62.refs_2_), channel_id=1, source_target_pairs={{0,4},{1,5},{2,6},{3,7},{4,0},{5,1},{6,2},{7,3},{8,12},{9,13},{10,... | collective-permute-start | bytes 4325384 | tf_op jit(solution)/shard_map/ppermute | solution.py:156
  455.4 63.3 %collective-permute-start.67 = (bf16[1408,512]{1,0:T(8,128)(2,1)S(1)}, bf16[1408,512]{1,0:T(8,128)(2,1)S(1)}, u32[]{:S(2)}, u32[]{:S(2)}) collective-permute-start(bf16[1408,512]{1,0:T(8,128)(2,1)S(1)} %get-tuple-element.357.refs_0_), channel_id=1, source_target_pairs={{0,4},{1,5},{2,6},{3,7},{4,0},{5,1},{6,2},{7,3},{8,12},{9,13},{10,... | collective-permute-start | bytes 4325384 | tf_op jit(solution)/shard_map/ppermute | solution.py:156
  (87 other events, 1422.5 us)

commit v4 on v3

--- a/solution.py
+++ b/solution.py
@@ -53,11 +53,13 @@
             begin += piece.shape[0]
         used += count
         groups.append(group)
-    for copy in copies + [c for group in groups for c in group]:
+    for copy in copies + groups[0]:
         copy.start()
     for copy in copies:
         copy.wait()
     for i, group in enumerate(groups):
+        for copy in groups[i + 1] if i + 1 < len(groups) else []:
+            copy.start()
         for copy in group:
             copy.wait()
         first = pl.multiple_of(at[i], 16)
@@ -107,11 +109,11 @@
     out[0] = total if first else total + refs[n_pieces][0]
 
 
-def add_block(out, shape, place, scaled, pieces, part, first):
+def add_block(out, shape, place, scaled, pieces, part, first, tiles=2):
     freqs, rows, _ = scaled.shape
     cols, width = pieces[0].shape
     depth = width * len(pieces)
-    tile = rows // 2
+    tile = rows // tiles
     block = pl.BlockSpec((1, tile, cols), lambda f, i, p: (f, i, p[0]))
     in_specs = [pl.BlockSpec((1, tile, depth), lambda f, i, p: (f, i, part))]
     in_specs += [pl.BlockSpec((cols, width), lambda f, i, p: (0, 0))] * len(pieces)
@@ -124,7 +126,7 @@
         functools.partial(block_kernel, n_pieces=len(pieces), first=first),
         out_shape=jax.ShapeDtypeStruct(shape, F32),
         grid_spec=pltpu.PrefetchScalarGridSpec(
-            num_scalar_prefetch=1, grid=(freqs, 2), in_specs=in_specs, out_specs=block
+            num_scalar_prefetch=1, grid=(freqs, tiles), in_specs=in_specs, out_specs=block
         ),
         input_output_aliases=aliases,
         compiler_params=pltpu.CompilerParams(vmem_limit_bytes=56 * 2**20),
@@ -216,7 +218,7 @@
     def cross_k(n):
         return {f"kcross{n}": over_k(env[f"cross{n}"])}
 
-    cuts = [slab_rows * i // SLAB_PARTS // 16 * 16 for i in range(SLAB_PARTS)] + [slab_rows]
+    cuts = [slab_rows * i // 11 // 16 * 16 for i in (0, 3, 7)] + [slab_rows]
 
     def slab_part(i):
         return {f"slab_x{i}": over_x(env["slab"][:cuts[1]] if i == 0 else env.pop(f"slab{i}"))}
@@ -291,15 +293,20 @@
     def cross_core(*names):
         return {f"k{name}": over_k(env[name]) for name in names}
 
-    def block(s, crossed, new):
+    def block(s, crossed, new, half=None):
         env.update(new)
         near = 1 - s % 2
         plane = jnp.where(u == 0, 1 - near, near)
         plane = jnp.where(x == 0, plane, 1 - plane)
         place = plane * 2 + (1 - y if crossed else y)
         names = [f"{q}{p}{s}" for p in (("yo", "yc") if crossed else ("o", "c")) for q in ("", "k")]
+        if half is not None:
+            names = names[2 * half : 2 * half + 2]
         pieces = [env.pop(n) if crossed or n[0] == "k" else env[n] for n in names]
-        env["out"] = add_block(env.get("out"), shape, place, env[f"scaled{s // 2}"], pieces, 0, s < 2)
+        first = s < 2 and not half
+        env["out"] = add_block(
+            env.get("out"), shape, place, env[f"scaled{s // 2}"], pieces, half or 0, first, 2 if half is None else 4
+        )
 
     env["coef"], env["slab"] = coef, half_slab
     parts = {f"slab{i}": env["slab"][cuts[i] : cuts[i + 1]] for i in range(1, SLAB_PARTS)}
@@ -319,15 +326,16 @@
     step(**first, **transformed(1))
     step(**inward(1), **outward(0), **own_x(1), **cross_core("own1", "own_x0"))
     r = choose(0) | cross_y("o0") | cross_core("o0", "own_x1")
-    step(**r, **inward(2), **exchange(1), **panel(0))
+    env.update({n: r.pop(n) for n in ("kown_x1",)})
+    step(**r, **exchange(1), **panel(0), **panel(1))
     join(0)
-    r = cross_y("c0") | inward(3) | outward(1) | cross_core("yo0")
+    r = cross_y("c0") | inward(2) | outward(1) | cross_core("yo0")
     block(0, False, cross_core("c0"))
     step(**r)
-    r = choose(1) | cross_y("o1") | outward(2) | cross_core("o1")
+    r = choose(1) | cross_y("o1") | inward(3) | outward(2) | cross_core("o1")
     block(0, True, cross_core("yc0"))
     step(**r)
-    r = choose(2) | cross_y("c1") | outward(3) | cross_core("o2", "yo1") | panel(1)
+    r = choose(2) | cross_y("c1") | outward(3) | cross_core("o2", "yo1")
     block(1, False, cross_core("c1"))
     step(**r)
     join(2)

time: 551 us -> 550 us (level)
  transfers between devices with their start and end apart: 71 -> 71, of which waited for: 29 -> 30; matrix products, arithmetic and copies ran while one was open for 6% -> 7% of each run, Pallas kernels for 28% -> 28%
where the time goes in v4:
time: 550 us; the launch traced here: 544 us
  waiting for transfers between devices  246 us (45%)
  Pallas kernels  183 us (33%)
  starting transfers between devices  67.6 us (12%)
  other arithmetic  32.1 us (6%)
  local copies, waits for them, and re-layouts  13.4 us (2%)
    ppermute x71, waiting for transfers between devices, move(): return lax.ppermute(array, AXES, pairs)  246 us
    pallas_call x8, Pallas kernels, add_block(): pl.pallas_call(functools.partial(block_kernel, n_pieces=len(pieces), firs...  158 us
    ppermute x71, starting transfers between devices, move(): return lax.ppermute(array, AXES, pairs)  67.6 us
    pallas_call x2, Pallas kernels, transform(): pl.pallas_call(functools.partial(transform_kernel, counts=[len(g) for g i...  25.5 us
  transfers between devices with their start and end apart: 71, of which 30 were waited for; matrix products, arithmetic and copies ran while one was open for 7% of the time, Pallas kernels for 28%

profile of v4, /device:TPU:2, one launch (start us, length us, event | category | flops | bytes accessed | tf_op | source)
XLA Modules:
  0.0 544.1 jit_solution(11282441308076253536)
XLA Ops:
  9.3 14.2 %collective-permute-done.4.refs_2_ = bf16[96,4608]{1,0:T(8,128)(2,1)} collective-permute-done((bf16[96,4608]{1,0:T(8,128)(2,1)S(1)}, bf16[96,4608]{1,0:T(8,128)(2,1)}, u32[]{:S(2)}, u32[]{:S(2)}) %collective-permute-start.4) | collective-permute-done | bytes 884768 | tf_op jit(solution)/shard_map/ppermute | solution.py:158
  45.1 26.3 %collective-permute-done.7 = bf16[288,2048]{1,0:T(8,128)(2,1)} collective-permute-done((bf16[288,2048]{1,0:T(8,128)(2,1)}, bf16[288,2048]{1,0:T(8,128)(2,1)}, u32[]{:S(2)}, u32[]{:S(2)}) %collective-permute-start.7) | collective-permute-done | bytes 1179680 | tf_op jit(solution)/shard_map/ppermute | solution.py:158
  80.7 24.2 %collective-permute-done.14 = bf16[288,2048]{1,0:T(8,128)(2,1)} collective-permute-done((bf16[288,2048]{1,0:T(8,128)(2,1)}, bf16[288,2048]{1,0:T(8,128)(2,1)}, u32[]{:S(2)}, u32[]{:S(2)}) %collective-permute-start.14) | collective-permute-done | bytes 1179680 | tf_op jit(solution)/shard_map/ppermute | solution.py:158
  112.7 14.4 %collective-permute-done.20.refs_22_ = bf16[288,1024]{1,0:T(8,128)(2,1)} collective-permute-done((bf16[288,1024]{1,0:T(8,128)(2,1)S(1)}, bf16[288,1024]{1,0:T(8,128)(2,1)}, u32[]{:S(2)}, u32[]{:S(2)}) %collective-permute-start.20) | collective-permute-done | bytes 589856 | tf_op jit(solution)/shard_map/ppermute | solution.py:158
  130.6 12.8 %shard_map.55 = bf16[1408,512]{1,0:T(8,128)(2,1)} custom-call(s32[36]{0:T(128)} %stack.69.at, bf16[352,4608]{1,0:T(8,128)(2,1)} %refs_0_.1, bf16[352,4608]{1,0:T(8,128)(2,1)} %collective-permute-done.5.refs_1_, bf16[96,4608]{1,0:T(8,128)(2,1)} %collective-permute-done.4.refs_2_, bf16[128,4608]{1,0:T(8,128)(2,1)} %collective-permute-done.10.refs_3_, ...), custom_call_target="tpu_custom_call" | custom-call | flops 6643777536 | bytes 17694720 | tf_op jit(solution)/shard_map/pallas_call | solution.py:76
  146.6 6.0 %collective-permute-start.28 = (bf16[1408,512]{1,0:T(8,128)(2,1)}, bf16[1408,512]{1,0:T(8,128)(2,1)}, u32[]{:S(2)}, u32[]{:S(2)}) collective-permute-start(bf16[1408,512]{1,0:T(8,128)(2,1)} %shard_map.55), channel_id=1, source_target_pairs={{0,8},{1,9},{2,10},{3,11},{4,12},{5,13},{6,14},{7,15},{8,0},{9,1},... | collective-permute-start | bytes 4325384 | tf_op jit(solution)/shard_map/ppermute | solution.py:158
  161.6 12.7 %shard_map.56 = bf16[1408,512]{1,0:T(8,128)(2,1)} custom-call(s32[36]{0:T(128)} %stack.71.at, bf16[352,4608]{1,0:T(8,128)(2,1)} %refs_0_.1, bf16[352,4608]{1,0:T(8,128)(2,1)} %collective-permute-done.5.refs_1_, bf16[96,4608]{1,0:T(8,128)(2,1)} %collective-permute-done.4.refs_2_, bf16[128,4608]{1,0:T(8,128)(2,1)} %collective-permute-done.10.refs_3_, ...), custom_call_target="tpu_custom_call" | custom-call | flops 6643777536 | bytes 17694720 | tf_op jit(solution)/shard_map/pallas_call | solution.py:76
  174.4 9.9 %collective-permute-done.28 = bf16[1408,512]{1,0:T(8,128)(2,1)} collective-permute-done((bf16[1408,512]{1,0:T(8,128)(2,1)}, bf16[1408,512]{1,0:T(8,128)(2,1)}, u32[]{:S(2)}, u32[]{:S(2)}) %collective-permute-start.28) | collective-permute-done | bytes 1441824 | tf_op jit(solution)/shard_map/ppermute | solution.py:158
  192.0 29.6 %collective-permute-done.32 = bf16[1408,512]{1,0:T(8,128)(2,1)} collective-permute-done((bf16[1408,512]{1,0:T(8,128)(2,1)}, bf16[1408,512]{1,0:T(8,128)(2,1)}, u32[]{:S(2)}, u32[]{:S(2)}) %collective-permute-start.32) | collective-permute-done | bytes 1441824 | tf_op jit(solution)/shard_map/ppermute | solution.py:158
  245.6 14.2 %collective-permute-done.36 = bf16[1408,512]{1,0:T(8,128)(2,1)S(1)} collective-permute-done((bf16[1408,512]{1,0:T(8,128)(2,1)S(1)}, bf16[1408,512]{1,0:T(8,128)(2,1)S(1)}, u32[]{:S(2)}, u32[]{:S(2)}) %collective-permute-start.36) | collective-permute-done | bytes 1441824 | tf_op jit(solution)/shard_map/ppermute | solution.py:158
  265.7 19.2 %shard_map.57.refs_4_ = f32[3,704,5632]{2,1,0:T(8,128)} custom-call(s32[1]{0:T(128)} %bitcast.24.place, bf16[3,704,2048]{2,1,0:T(8,128)(2,1)} %pad_maximum_fusion.scaled, bf16[1408,512]{1,0:T(8,128)(2,1)} %copy-done.7, bf16[1408,512]{1,0:T(8,128)(2,1)} %copy-done.22, bf16[1408,512]{1,0:T(8,128)(2,1)} %copy-done.6, ...), custom_call_target="tpu_custom_call" | custom-call | flops 12180258816 | bytes 26312704 | tf_op jit(solution)/shard_map/pallas_call | solution.py:125
  284.9 10.2 %collective-permute-done.42.refs_2_ = bf16[1408,512]{1,0:T(8,128)(2,1)} collective-permute-done((bf16[1408,512]{1,0:T(8,128)(2,1)S(1)}, bf16[1408,512]{1,0:T(8,128)(2,1)}, u32[]{:S(2)}, u32[]{:S(2)}) %collective-permute-start.42) | collective-permute-done | bytes 1441824 | tf_op jit(solution)/shard_map/ppermute | solution.py:158
  295.1 7.9 %collective-permute-done.44 = bf16[1408,512]{1,0:T(8,128)(2,1)} collective-permute-done((bf16[1408,512]{1,0:T(8,128)(2,1)}, bf16[1408,512]{1,0:T(8,128)(2,1)}, u32[]{:S(2)}, u32[]{:S(2)}) %collective-permute-start.44) | collective-permute-done | bytes 1441824 | tf_op jit(solution)/shard_map/ppermute | solution.py:158
  310.7 19.2 %shard_map.58.refs_4_ = f32[3,704,5632]{2,1,0:T(8,128)} custom-call(s32[1]{0:T(128)} %bitcast.25.place, bf16[3,704,2048]{2,1,0:T(8,128)(2,1)} %pad_maximum_fusion.scaled, bf16[1408,512]{1,0:T(8,128)(2,1)} %collective-permute-done.37.refs_0_, bf16[1408,512]{1,0:T(8,128)(2,1)} %collective-permute-done.45.refs_1_, ...), custom_call_target="tpu_custom_call", output_to_operand_aliasing={{}: (6, {})} | custom-call | flops 12180258816 | bytes 26312704 | tf_op jit(solution)/shard_map/pallas_call | solution.py:125
  329.9 10.6 %collective-permute-done.47.refs_2_ = bf16[1408,512]{1,0:T(8,128)(2,1)} collective-permute-done((bf16[1408,512]{1,0:T(8,128)(2,1)}, bf16[1408,512]{1,0:T(8,128)(2,1)}, u32[]{:S(2)}, u32[]{:S(2)}) %collective-permute-start.47) | collective-permute-done | bytes 1441824 | tf_op jit(solution)/shard_map/ppermute | solution.py:158
  352.4 19.1 %shard_map.59.refs_4_ = f32[3,704,5632]{2,1,0:T(8,128)} custom-call(s32[1]{0:T(128)} %bitcast.26.place, bf16[3,704,2048]{2,1,0:T(8,128)(2,1)} %pad_maximum_fusion.scaled, bf16[1408,512]{1,0:T(8,128)(2,1)} %copy-done.9, bf16[1408,512]{1,0:T(8,128)(2,1)} %collective-permute-done.51.refs_1_, ...), custom_call_target="tpu_custom_call", output_to_operand_aliasing={{}: (6, {})} | custom-call | flops 12180258816 | bytes 26312704 | tf_op jit(solution)/shard_map/pallas_call | solution.py:125
  371.6 13.3 %collective-permute-done.53 = bf16[1408,512]{1,0:T(8,128)(2,1)S(1)} collective-permute-done((bf16[1408,512]{1,0:T(8,128)(2,1)}, bf16[1408,512]{1,0:T(8,128)(2,1)S(1)}, u32[]{:S(2)}, u32[]{:S(2)}) %collective-permute-start.53) | collective-permute-done | bytes 1441824 | tf_op jit(solution)/shard_map/ppermute | solution.py:158
  395.0 19.2 %shard_map.60.refs_4_ = f32[3,704,5632]{2,1,0:T(8,128)} custom-call(s32[1]{0:T(128)} %bitcast.place, bf16[3,704,2048]{2,1,0:T(8,128)(2,1)} %pad_maximum_fusion.scaled, bf16[1408,512]{1,0:T(8,128)(2,1)} %collective-permute-done.48.refs_0_, bf16[1408,512]{1,0:T(8,128)(2,1)} %collective-permute-done.57.refs_1_, ...), custom_call_target="tpu_custom_call", output_to_operand_aliasing={{}: (6, {})} | custom-call | flops 12180258816 | bytes 26312704 | tf_op jit(solution)/shard_map/pallas_call | solution.py:125
  414.1 20.3 %shard_map.61.refs_4_ = f32[3,704,5632]{2,1,0:T(8,128)} custom-call(s32[1]{0:T(128)} %bitcast.24.place, bf16[3,704,2048]{2,1,0:T(8,128)(2,1)} %pad_maximum_fusion.1.scaled, bf16[1408,512]{1,0:T(8,128)(2,1)} %copy-done.8, bf16[1408,512]{1,0:T(8,128)(2,1)} %collective-permute-done.56.refs_1_, ...), custom_call_target="tpu_custom_call", output_to_operand_aliasing={{}: (6, {})} | custom-call | flops 12180258816 | bytes 38207488 | tf_op jit(solution)/shard_map/pallas_call | solution.py:125
  434.5 17.1 %collective-permute-done.60.refs_0_ = bf16[1408,512]{1,0:T(8,128)(2,1)} collective-permute-done((bf16[1408,512]{1,0:T(8,128)(2,1)S(1)}, bf16[1408,512]{1,0:T(8,128)(2,1)}, u32[]{:S(2)}, u32[]{:S(2)}) %collective-permute-start.60) | collective-permute-done | bytes 1441824 | tf_op jit(solution)/shard_map/ppermute | solution.py:158
  456.5 20.3 %shard_map.62.refs_4_ = f32[3,704,5632]{2,1,0:T(8,128)} custom-call(s32[1]{0:T(128)} %bitcast.26.place, bf16[3,704,2048]{2,1,0:T(8,128)(2,1)} %pad_maximum_fusion.1.scaled, bf16[1408,512]{1,0:T(8,128)(2,1)} %copy-done.10, bf16[1408,512]{1,0:T(8,128)(2,1)} %collective-permute-done.63.refs_1_, ...), custom_call_target="tpu_custom_call", output_to_operand_aliasing={{}: (6, {})} | custom-call | flops 12180258816 | bytes 38207488 | tf_op jit(solution)/shard_map/pallas_call | solution.py:125
  477.9 20.3 %shard_map.63.refs_4_ = f32[3,704,5632]{2,1,0:T(8,128)} custom-call(s32[1]{0:T(128)} %bitcast.25.place, bf16[3,704,2048]{2,1,0:T(8,128)(2,1)} %pad_maximum_fusion.1.scaled, bf16[1408,512]{1,0:T(8,128)(2,1)} %collective-permute-done.60.refs_0_, bf16[1408,512]{1,0:T(8,128)(2,1)} %copy-done.26, ...), custom_call_target="tpu_custom_call", output_to_operand_aliasing={{}: (6, {})} | custom-call | flops 12180258816 | bytes 38207488 | tf_op jit(solution)/shard_map/pallas_call | solution.py:125
  498.2 19.1 %collective-permute-done.67.refs_0_ = bf16[1408,512]{1,0:T(8,128)(2,1)S(1)} collective-permute-done((bf16[1408,512]{1,0:T(8,128)(2,1)S(1)}, bf16[1408,512]{1,0:T(8,128)(2,1)S(1)}, u32[]{:S(2)}, u32[]{:S(2)}) %collective-permute-start.67) | collective-permute-done | bytes 1441824 | tf_op jit(solution)/shard_map/ppermute | solution.py:158
  523.8 20.3 %shard_map.64 = f32[3,704,5632]{2,1,0:T(8,128)} custom-call(s32[1]{0:T(128)} %bitcast.place, bf16[3,704,2048]{2,1,0:T(8,128)(2,1)} %pad_maximum_fusion.1.scaled, bf16[1408,512]{1,0:T(8,128)(2,1)} %copy-done.25, bf16[1408,512]{1,0:T(8,128)(2,1)} %copy-done.27, bf16[1408,512]{1,0:T(8,128)(2,1)} %copy-done.24, ...), custom_call_target="tpu_custom_call", output_to_operand_aliasing={{}: (6, {})} | custom-call | flops 12180258816 | bytes 38207488 | tf_op jit(solution)/shard_map/pallas_call | solution.py:125
  (231 shorter events, 142.2 us)
Async XLA Ops:
  0.0 37.2 %collective-permute-start.5 = (bf16[352,4608]{1,0:T(8,128)(2,1)}, bf16[352,4608]{1,0:T(8,128)(2,1)}, u32[]{:S(2)}, u32[]{:S(2)}) collective-permute-start(bf16[352,4608]{1,0:T(8,128)(2,1)} %refs_0_.1), channel_id=1, source_target_pairs={{0,2},{1,3},{2,0},{3,1},{4,6},{5,7},{6,4},{7,5},{8,10},{9,11},{10,... | collective-permute-start | bytes 9732104 | tf_op jit(solution)/shard_map/ppermute | solution.py:158
  146.6 37.7 %collective-permute-start.28 = (bf16[1408,512]{1,0:T(8,128)(2,1)}, bf16[1408,512]{1,0:T(8,128)(2,1)}, u32[]{:S(2)}, u32[]{:S(2)}) collective-permute-start(bf16[1408,512]{1,0:T(8,128)(2,1)} %shard_map.55), channel_id=1, source_target_pairs={{0,8},{1,9},{2,10},{3,11},{4,12},{5,13},{6,14},{7,15},{8,0},{9,1},... | collective-permute-start | bytes 4325384 | tf_op jit(solution)/shard_map/ppermute | solution.py:158
  187.6 34.0 %collective-permute-start.32 = (bf16[1408,512]{1,0:T(8,128)(2,1)}, bf16[1408,512]{1,0:T(8,128)(2,1)}, u32[]{:S(2)}, u32[]{:S(2)}) collective-permute-start(bf16[1408,512]{1,0:T(8,128)(2,1)} %collective-permute-done.27), channel_id=1, source_target_pairs={{8,0},{9,1},{10,2},{11,3},{12,4},{13,5},{14,6},{15,7},{16,24},{17,... | collective-permute-start | bytes 4325384 | tf_op jit(solution)/shard_map/ppermute | solution.py:158
  223.2 36.6 %collective-permute-start.37 = (bf16[1408,512]{1,0:T(8,128)(2,1)S(1)}, bf16[1408,512]{1,0:T(8,128)(2,1)}, u32[]{:S(2)}, u32[]{:S(2)}) collective-permute-start(bf16[1408,512]{1,0:T(8,128)(2,1)S(1)} %get-tuple-element.298.refs_0_), channel_id=1, source_target_pairs={{0,4},{1,5},{2,6},{3,7},{4,0},{5,1},{6,2},{7,3},{8,12},{9,13},{10,... | collective-permute-start | bytes 4325384 | tf_op jit(solution)/shard_map/ppermute | solution.py:158
  224.0 35.9 %collective-permute-start.38 = (bf16[1408,512]{1,0:T(8,128)(2,1)S(1)}, bf16[1408,512]{1,0:T(8,128)(2,1)S(1)}, u32[]{:S(2)}, u32[]{:S(2)}) collective-permute-start(bf16[1408,512]{1,0:T(8,128)(2,1)S(1)} %get-tuple-element.298.refs_0_), channel_id=1, source_target_pairs={{0,2},{1,3},{2,0},{3,1},{4,6},{5,7},{6,4},{7,5},{8,10},{9,11},{10,... | collective-permute-start | bytes 4325384 | tf_op jit(solution)/shard_map/ppermute | solution.py:158
  224.0 35.9 %collective-permute-start.36 = (bf16[1408,512]{1,0:T(8,128)(2,1)S(1)}, bf16[1408,512]{1,0:T(8,128)(2,1)S(1)}, u32[]{:S(2)}, u32[]{:S(2)}) collective-permute-start(bf16[1408,512]{1,0:T(8,128)(2,1)S(1)} %get-tuple-element.358), channel_id=1, source_target_pairs={{0,1},{2,3},{4,5},{6,7},{8,9},{10,11},{12,13},{14,15},{17,16},{19,... | collective-permute-start | bytes 4325384 | tf_op jit(solution)/shard_map/ppermute | solution.py:158
  225.3 35.3 %collective-permute-start.39 = (bf16[1408,512]{1,0:T(8,128)(2,1)S(1)}, bf16[1408,512]{1,0:T(8,128)(2,1)}, u32[]{:S(2)}, u32[]{:S(2)}) collective-permute-start(bf16[1408,512]{1,0:T(8,128)(2,1)S(1)} %copy-done.3), channel_id=1, source_target_pairs={{0,8},{1,9},{2,10},{3,11},{4,12},{5,13},{6,14},{7,15},{8,0},{9,1},... | collective-permute-start | bytes 4325384 | tf_op jit(solution)/shard_map/ppermute | solution.py:158
  261.0 34.1 %collective-permute-start.42 = (bf16[1408,512]{1,0:T(8,128)(2,1)S(1)}, bf16[1408,512]{1,0:T(8,128)(2,1)}, u32[]{:S(2)}, u32[]{:S(2)}) collective-permute-start(bf16[1408,512]{1,0:T(8,128)(2,1)S(1)} %broadcast_select_fusion.10.refs_2_), channel_id=1, source_target_pairs={{0,4},{1,5},{2,6},{3,7},{4,0},{5,1},{6,2},{7,3},{8,12},{9,13},{10,... | collective-permute-start | bytes 4325384 | tf_op jit(solution)/shard_map/ppermute | solution.py:158
  264.1 38.9 %collective-permute-start.44 = (bf16[1408,512]{1,0:T(8,128)(2,1)}, bf16[1408,512]{1,0:T(8,128)(2,1)}, u32[]{:S(2)}, u32[]{:S(2)}) collective-permute-start(bf16[1408,512]{1,0:T(8,128)(2,1)} %collective-permute-done.31), channel_id=1, source_target_pairs={{8,0},{9,1},{10,2},{11,3},{12,4},{13,5},{14,6},{15,7},{16,24},{17,... | collective-permute-start | bytes 4325384 | tf_op jit(solution)/shard_map/ppermute | solution.py:158
  265.4 37.6 %collective-permute-start.45 = (bf16[1408,512]{1,0:T(8,128)(2,1)}, bf16[1408,512]{1,0:T(8,128)(2,1)}, u32[]{:S(2)}, u32[]{:S(2)}) collective-permute-start(bf16[1408,512]{1,0:T(8,128)(2,1)} %collective-permute-done.37.refs_0_), channel_id=1, source_target_pairs={{0,2},{1,3},{2,0},{3,1},{4,6},{5,7},{6,4},{7,5},{8,10},{9,11},{10,... | collective-permute-start | bytes 4325384 | tf_op jit(solution)/shard_map/ppermute | solution.py:158
  306.2 34.3 %collective-permute-start.47 = (bf16[1408,512]{1,0:T(8,128)(2,1)}, bf16[1408,512]{1,0:T(8,128)(2,1)}, u32[]{:S(2)}, u32[]{:S(2)}) collective-permute-start(bf16[1408,512]{1,0:T(8,128)(2,1)} %get-tuple-element.361), channel_id=1, source_target_pairs={{0,1},{1,0},{2,3},{3,2},{4,5},{5,4},{6,7},{7,6},{8,9},{9,8},{10,11... | collective-permute-start | bytes 4325384 | tf_op jit(solution)/shard_map/ppermute | solution.py:158
  309.3 35.6 %collective-permute-start.50 = (bf16[1408,512]{1,0:T(8,128)(2,1)}, bf16[1408,512]{1,0:T(8,128)(2,1)}, u32[]{:S(2)}, u32[]{:S(2)}) collective-permute-start(bf16[1408,512]{1,0:T(8,128)(2,1)} %collective-permute-done.43), channel_id=1, source_target_pairs={{8,0},{9,1},{10,2},{11,3},{12,4},{13,5},{14,6},{15,7},{16,24},{17,... | collective-permute-start | bytes 4325384 | tf_op jit(solution)/shard_map/ppermute | solution.py:158
  310.6 34.3 %collective-permute-start.51 = (bf16[1408,512]{1,0:T(8,128)(2,1)S(1)}, bf16[1408,512]{1,0:T(8,128)(2,1)}, u32[]{:S(2)}, u32[]{:S(2)}) collective-permute-start(bf16[1408,512]{1,0:T(8,128)(2,1)S(1)} %get-tuple-element.323.refs_0_), channel_id=1, source_target_pairs={{0,2},{1,3},{2,0},{3,1},{4,6},{5,7},{6,4},{7,5},{8,10},{9,11},{10,... | collective-permute-start | bytes 4325384 | tf_op jit(solution)/shard_map/ppermute | solution.py:158
  345.0 39.9 %collective-permute-start.54 = (bf16[1408,512]{1,0:T(8,128)(2,1)}, bf16[1408,512]{1,0:T(8,128)(2,1)}, u32[]{:S(2)}, u32[]{:S(2)}) collective-permute-start(bf16[1408,512]{1,0:T(8,128)(2,1)} %collective-permute-done.47.refs_2_), channel_id=1, source_target_pairs={{0,4},{1,5},{2,6},{3,7},{4,0},{5,1},{6,2},{7,3},{8,12},{9,13},{10,... | collective-permute-start | bytes 4325384 | tf_op jit(solution)/shard_map/ppermute | solution.py:158
  349.0 35.8 %collective-permute-start.53 = (bf16[1408,512]{1,0:T(8,128)(2,1)}, bf16[1408,512]{1,0:T(8,128)(2,1)S(1)}, u32[]{:S(2)}, u32[]{:S(2)}) collective-permute-start(bf16[1408,512]{1,0:T(8,128)(2,1)} %get-tuple-element.356), channel_id=1, source_target_pairs={{0,1},{2,3},{4,5},{6,7},{8,9},{10,11},{12,13},{14,15},{17,16},{19,... | collective-permute-start | bytes 4325384 | tf_op jit(solution)/shard_map/ppermute | solution.py:158
  350.3 35.9 %collective-permute-start.55 = (bf16[1408,512]{1,0:T(8,128)(2,1)}, bf16[1408,512]{1,0:T(8,128)(2,1)}, u32[]{:S(2)}, u32[]{:S(2)}) collective-permute-start(bf16[1408,512]{1,0:T(8,128)(2,1)} %collective-permute-done.49), channel_id=1, source_target_pairs={{8,0},{9,1},{10,2},{11,3},{12,4},{13,5},{14,6},{15,7},{16,24},{17,... | collective-permute-start | bytes 4325384 | tf_op jit(solution)/shard_map/ppermute | solution.py:158
  351.8 34.4 %collective-permute-start.56 = (bf16[1408,512]{1,0:T(8,128)(2,1)S(1)}, bf16[1408,512]{1,0:T(8,128)(2,1)}, u32[]{:S(2)}, u32[]{:S(2)}) collective-permute-start(bf16[1408,512]{1,0:T(8,128)(2,1)S(1)} %get-tuple-element.335.refs_0_), channel_id=1, source_target_pairs={{0,2},{1,3},{2,0},{3,1},{4,6},{5,7},{6,4},{7,5},{8,10},{9,11},{10,... | collective-permute-start | bytes 4325384 | tf_op jit(solution)/shard_map/ppermute | solution.py:158
  352.1 34.1 %collective-permute-start.57 = (bf16[1408,512]{1,0:T(8,128)(2,1)}, bf16[1408,512]{1,0:T(8,128)(2,1)}, u32[]{:S(2)}, u32[]{:S(2)}) collective-permute-start(bf16[1408,512]{1,0:T(8,128)(2,1)} %collective-permute-done.48.refs_0_), channel_id=1, source_target_pairs={{0,2},{1,3},{2,0},{3,1},{4,6},{5,7},{6,4},{7,5},{8,10},{9,11},{10,... | collective-permute-start | bytes 4325384 | tf_op jit(solution)/shard_map/ppermute | solution.py:158
  387.0 64.6 %collective-permute-start.61 = (bf16[1408,512]{1,0:T(8,128)(2,1)S(1)}, bf16[1408,512]{1,0:T(8,128)(2,1)S(1)}, u32[]{:S(2)}, u32[]{:S(2)}) collective-permute-start(bf16[1408,512]{1,0:T(8,128)(2,1)S(1)} %broadcast_select_fusion.6.refs_2_), channel_id=1, source_target_pairs={{0,4},{1,5},{2,6},{3,7},{4,0},{5,1},{6,2},{7,3},{8,12},{9,13},{10,... | collective-permute-start | bytes 4325384 | tf_op jit(solution)/shard_map/ppermute | solution.py:158
  387.7 63.9 %collective-permute-start.60 = (bf16[1408,512]{1,0:T(8,128)(2,1)S(1)}, bf16[1408,512]{1,0:T(8,128)(2,1)}, u32[]{:S(2)}, u32[]{:S(2)}) collective-permute-start(bf16[1408,512]{1,0:T(8,128)(2,1)S(1)} %get-tuple-element.335.refs_0_), channel_id=1, source_target_pairs={{0,4},{1,5},{2,6},{3,7},{4,0},{5,1},{6,2},{7,3},{8,12},{9,13},{10,... | collective-permute-start | bytes 4325384 | tf_op jit(solution)/shard_map/ppermute | solution.py:158
  391.1 60.5 %collective-permute-start.62 = (bf16[1408,512]{1,0:T(8,128)(2,1)S(1)}, bf16[1408,512]{1,0:T(8,128)(2,1)}, u32[]{:S(2)}, u32[]{:S(2)}) collective-permute-start(bf16[1408,512]{1,0:T(8,128)(2,1)S(1)} %get-tuple-element.359), channel_id=1, source_target_pairs={{0,1},{1,0},{2,3},{3,2},{4,5},{5,4},{6,7},{7,6},{8,9},{9,8},{10,11... | collective-permute-start | bytes 4325384 | tf_op jit(solution)/shard_map/ppermute | solution.py:158
  395.0 56.6 %collective-permute-start.63 = (bf16[1408,512]{1,0:T(8,128)(2,1)S(1)}, bf16[1408,512]{1,0:T(8,128)(2,1)}, u32[]{:S(2)}, u32[]{:S(2)}) collective-permute-start(bf16[1408,512]{1,0:T(8,128)(2,1)S(1)} %get-tuple-element.347.refs_0_), channel_id=1, source_target_pairs={{0,2},{1,3},{2,0},{3,1},{4,6},{5,7},{6,4},{7,5},{8,10},{9,11},{10,... | collective-permute-start | bytes 4325384 | tf_op jit(solution)/shard_map/ppermute | solution.py:158
  452.2 65.0 %collective-permute-start.68 = (bf16[1408,512]{1,0:T(8,128)(2,1)}, bf16[1408,512]{1,0:T(8,128)(2,1)S(1)}, u32[]{:S(2)}, u32[]{:S(2)}) collective-permute-start(bf16[1408,512]{1,0:T(8,128)(2,1)} %collective-permute-done.62.refs_2_), channel_id=1, source_target_pairs={{0,4},{1,5},{2,6},{3,7},{4,0},{5,1},{6,2},{7,3},{8,12},{9,13},{10,... | collective-permute-start | bytes 4325384 | tf_op jit(solution)/shard_map/ppermute | solution.py:158
  452.9 64.4 %collective-permute-start.67 = (bf16[1408,512]{1,0:T(8,128)(2,1)S(1)}, bf16[1408,512]{1,0:T(8,128)(2,1)S(1)}, u32[]{:S(2)}, u32[]{:S(2)}) collective-permute-start(bf16[1408,512]{1,0:T(8,128)(2,1)S(1)} %get-tuple-element.347.refs_0_), channel_id=1, source_target_pairs={{0,4},{1,5},{2,6},{3,7},{4,0},{5,1},{6,2},{7,3},{8,12},{9,13},{10,... | collective-permute-start | bytes 4325384 | tf_op jit(solution)/shard_map/ppermute | solution.py:158
  (82 other events, 1455.1 us)
